TPU v7x, 128 devices: a whole 4x4x4 slice. The times are simulated.
128 devices in a mesh: freq: 8 (over z, x_lo), gx: 4 (over y), gy: 4 (over x_hi, core).
Axes of the slice: x: 4 (x_hi: 2, x_lo: 2; x = x_hi * 2 + x_lo), y: 4, z: 4, core: 2. Of those that a mesh axis runs over, the one named last changes fastest.
Arguments:
- wavefield: float32 [32, 2, 512, 512], P('freq', None, 'gx', 'gy'), may hold values from -6 to 6
- velocity: float32 [4, 512, 512], P(None, ('gx', 'freq'), 'gy'), may hold values from 1.5 to 4.5
Outputs:
- image: float32 [4, 512, 512], P(None, 'gx', 'gy')
- extrapolated: float32 [32, 2, 512, 512], P('freq', None, 'gx', 'gy')
All inputs are finite; a program needn't handle non-finite values.
Results may differ from a plain program's by a relative error of at most 0.0001.
Values sent between devices are 32-bit elements; how exact they have to be, the bound alone decides.
A program may use at most 128 MiB of HBM per device.

v0:
```python
import math

import jax
import jax.numpy as jnp
from jax import lax
from jax.sharding import PartitionSpec as P

ORDER = 8


lowest_freq = 2.0
highest_freq = 60.0
depth_interval = 0.01


def with_halo(cells, sides, width):
    for axis, dim in sides:
        count = lax.axis_size(axis)
        ends = count - 1
        head = lax.slice_in_dim(cells, 0, width, axis=dim)
        tail = lax.slice_in_dim(cells, cells.shape[dim] - width, cells.shape[dim], axis=dim)
        cells = jnp.concatenate(
            [
                lax.ppermute(tail, axis, [(i, (i + 1) % count) for i in range(ends)]),
                cells,
                lax.ppermute(head, axis, [((i + 1) % count, i) for i in range(ends)]),
            ],
            axis=dim,
        )
    return cells


def stencil(source):
    centre = source[..., 1:-1, 1:-1]
    along_x = source[..., 2:, 1:-1] + source[..., :-2, 1:-1]
    along_y = source[..., 1:-1, 2:] + source[..., 1:-1, :-2]
    diagonal_sum = (
        source[..., 2:, 2:] + source[..., 2:, :-2] + source[..., :-2, 2:] + source[..., :-2, :-2]
    )
    return -0.5 * centre + 0.25 * (along_x + along_y) + 0.125 * diagonal_sum


def neighbours(source):
    return stencil(with_halo(source, (("gx", 2), ("gy", 3)), 1))


def term_weights(order):
    values = [1.0 / (term + 1) for term in range(order + 1)]
    whole = sum(values)
    return [value / whole for value in values]


def add_term(real_part, imag_part, part, phase_base, term, weight, order):
    phase = phase_base * ((term + 1) / (order + 1))
    cosine = jnp.cos(phase)
    sine = jnp.sin(phase)
    real_part = real_part + weight * (cosine * part[:, 0] - sine * part[:, 1])
    imag_part = imag_part + weight * (sine * part[:, 0] + cosine * part[:, 1])
    return (real_part, imag_part)


def per_device(wavefield, velocity):
    order = ORDER
    weights = term_weights(order)
    freq_count = wavefield.shape[0]
    freq_total = freq_count * lax.axis_size("freq")
    freq_start = lax.axis_index("freq") * freq_count
    angular = (
        2.0
        * math.pi
        * (
            lowest_freq
            + (highest_freq - lowest_freq)
            * ((freq_start + jnp.arange(freq_count)).astype(jnp.float32) + 0.5)
            / freq_total
        )
    )
    wave_now = wavefield
    image_rows = []
    for depth in range(velocity.shape[0]):
        slowness_tile = lax.all_gather(velocity[depth], "freq", axis=0, tiled=True)
        phase_base = angular[:, None, None] * depth_interval / slowness_tile[None]
        zeros = jnp.zeros(wave_now[:, 0].shape, jnp.float32)
        real_part, imag_part = add_term(zeros, zeros, wave_now, phase_base, 0, weights[0], order)
        previous = wave_now
        present = neighbours(wave_now)
        real_part, imag_part = add_term(
            real_part, imag_part, present, phase_base, 1, weights[1], order
        )
        for term in range(2, order + 1):
            following = 2.0 * neighbours(present) - previous
            previous = present
            present = following
            real_part, imag_part = add_term(
                real_part, imag_part, present, phase_base, term, weights[term], order
            )
        wave_now = jnp.stack([real_part, imag_part], axis=1)
        partial_image = jnp.sum(real_part, axis=0)
        image_rows.append(lax.psum(partial_image, "freq") / math.sqrt(freq_total))
    image = jnp.stack(image_rows)
    return (image, wave_now)


def solution(mesh):
    placed = (P("freq", None, "gx", "gy"), P(None, ("gx", "freq"), "gy"))
    return jax.shard_map(
        per_device,
        mesh=mesh,
        in_specs=placed,
        out_specs=(P(None, "gx", "gy"), P("freq", None, "gx", "gy")),
        check_vma=False,
    )
```

profile of v0, /device:TPU:1, one launch (start us, length us, event | category | flops | bytes accessed | tf_op | source)
XLA Modules:
  0.0 1091.9 jit_solution(7510783588597941466)
XLA Ops:
  40.3 6.6 collective-permute-start.7
  60.8 6.2 collective-permute-start.11
  82.7 6.2 collective-permute-start.15
  103.5 6.6 collective-permute-start.19
  126.6 6.7 collective-permute-start.23
  150.3 6.0 collective-permute-start.27
  173.9 5.6 collective-permute-start.31
  179.5 23.5 %all-gather = f32[1,128,128]{2,1,0:T(8,128)S(1)} all-gather(f32[1,16,128]{2,1,0:T(8,128)S(1)} %get-tuple-element.213), channel_id=2, replica_groups=mesh['freq'=8,'gx'=4,'gy'=4] {'freq'}, dimensions={1}, use_global_device_ids=true | all-gather | bytes 73728 | tf_op jit(solution)/shard_map/all_gather | solution.py:81
  208.2 8.8 fusion.268
  217.1 8.9 fusion.273
  233.1 5.6 collective-permute-start.34
  239.0 6.1 collective-permute-start.35
  258.2 6.6 collective-permute-start.39
  278.2 6.6 collective-permute-start.43
  300.5 6.2 collective-permute-start.47
  321.3 6.6 collective-permute-start.51
  344.3 6.6 collective-permute-start.55
  367.8 6.2 collective-permute-start.59
  391.0 6.2 collective-permute-start.63
  397.2 22.1 %all-gather.1 = f32[1,128,128]{2,1,0:T(8,128)S(1)} all-gather(f32[1,16,128]{2,1,0:T(8,128)S(1)} %get-tuple-element.212), channel_id=3, replica_groups=mesh['freq'=8,'gx'=4,'gy'=4] {'freq'}, dimensions={1}, use_global_device_ids=true | all-gather | bytes 73728 | tf_op jit(solution)/shard_map/all_gather | solution.py:81
  424.7 8.8 fusion.278
  433.5 8.9 fusion.283
  457.9 6.5 collective-permute-start.67
  482.5 6.4 collective-permute-start.71
  508.9 5.7 collective-permute-start.75
  531.6 6.2 collective-permute-start.79
  555.1 6.2 collective-permute-start.83
  578.7 6.2 collective-permute-start.87
  602.3 6.2 collective-permute-start.91
  626.1 6.2 collective-permute-start.95
  632.3 24.1 %all-gather.2 = f32[1,128,128]{2,1,0:T(8,128)} all-gather(f32[1,16,128]{2,1,0:T(8,128)S(1)} %copy-done.107), channel_id=4, replica_groups=mesh['freq'=8,'gx'=4,'gy'=4] {'freq'}, dimensions={1}, use_global_device_ids=true | all-gather | bytes 73728 | tf_op jit(solution)/shard_map/all_gather | solution.py:81
  662.5 8.8 fusion.288
  671.4 8.9 fusion.331
  696.8 6.5 collective-permute-start.99
  723.0 5.8 collective-permute-start.103
  748.8 6.2 collective-permute-start.107
  775.0 5.4 collective-permute-start.111
  800.4 5.8 collective-permute-start.115
  826.2 5.8 collective-permute-start.119
  844.1 24.1 %all-gather.3 = f32[1,128,128]{2,1,0:T(8,128)} all-gather(f32[1,16,128]{2,1,0:T(8,128)S(1)} %copy-done.106), channel_id=5, replica_groups=mesh['freq'=8,'gx'=4,'gy'=4] {'freq'}, dimensions={1}, use_global_device_ids=true | all-gather | bytes 73728 | tf_op jit(solution)/shard_map/all_gather | solution.py:81
  878.6 8.1 collective-permute-start.123
  886.7 11.8 %fusion.539 = (f32[128,128]{1,0:T(8,128)}, f32[4,128,128]{2,1,0:T(8,128)}) fusion(f32[4,2,128,128]{3,2,0,1:T(8,128)} %copy-done.95, f32[4,2,128,128]{3,2,0,1:T(8,128)} %copy-done.65, f32[4,2,128,128]{3,2,0,1:T(8,128)} %copy-done.27, f32[4,2,128,128]{3,2,0,1:T(8,128)} %copy-done.25, f32[4,2,128,128]{3,2,0,1:T(8,128)} %copy-done.23, ...), kind=kLoop, calls=%fused_computation.1140 | loop fusion | flops 3522560 | bytes 5111824 | tf_op jit(solution)/shard_map/reduce_sum | solution.py:98
  913.1 21.5 %fusion.541 = (f32[128,128]{1,0:T(8,128)}, f32[4,128,128]{2,1,0:T(8,128)}, f32[4,128,128]{2,1,0:T(8,128)}) fusion(f32[4,2,128,128]{3,2,0,1:T(8,128)S(1)} %copy-done.92, f32[4,2,128,128]{3,2,0,1:T(8,128)S(1)} %copy-done.39, f32[4,2,128,128]{3,2,0,1:T(8,128)S(1)} %fusion.143, f32[4,2,128,128]{3,2,0,1:T(8,128)S(1)} %fusion.151, ...), kind=kLoop, calls=%fused_computation.1141 | loop fusion | flops 6995968 | bytes 9895952 | tf_op jit(solution)/shard_map/reduce_sum | solution.py:98
  949.6 24.2 %fusion.526 = (f32[128,128]{1,0:T(8,128)}, f32[4,128,128]{2,1,0:T(8,128)}) fusion(f32[4,128,128]{2,1,0:T(8,128)} %get-tuple-element.15, f32[4,2,128,128]{3,2,0,1:T(8,128)} %copy-done.93, f32[4,2,128,128]{3,2,0,1:T(8,128)} %copy-done.40, f32[4,2,128,128]{3,2,0,1:T(8,128)} %copy-done.15, f32[4,2,128,128]{3,2,0,1:T(8,128)} %copy-done.10, ...), kind=kLoop, calls=%fused_computation.1115 | loop fusion | flops 6995968 | bytes 9633808 | tf_op jit(solution)/shard_map/reduce_sum | solution.py:98
  981.8 9.5 fusion.263
  991.4 21.3 %fusion.295 = f32[128,128]{1,0:T(8,128)} fusion(f32[4,128,128]{2,1,0:T(8,128)S(1)} %copy-done.102, f32[4,128,128]{2,1,0:T(8,128)S(1)} %copy-done.98, f32[4,2,128,128]{3,2,0,1:T(8,128)S(1)} %fusion.3, f32[4,2,128,128]{3,2,0,1:T(8,128)S(1)} %copy-done.74, f32[4,2,128,128]{3,2,0,1:T(8,128)S(1)} %copy-done.61, f32[4,2,128,128]{3,2,0,1:T(8,128)S(1)} %copy-done.58, ...), kind=kLoop, calls=%fused_computation.640 | loop fusion | flops 9879552 | bytes 9109520 | tf_op jit(solution)/shard_map/reduce_sum | solution.py:98
  1014.2 10.6 fusion.255
  1025.7 56.6 %all-reduce.3.cloned.1.call-done = (f32[128,128]{0,1:T(8,128)}, f32[128,128]{0,1:T(8,128)}, f32[128,128]{0,1:T(8,128)}, f32[128,128]{0,1:T(8,128)}) async-done(((f32[128,128]{0,1:T(8,128)}, f32[128,128]{0,1:T(8,128)}, f32[128,128]{0,1:T(8,128)}, f32[128,128]{0,1:T(8,128)}), (f32[128,128]{0,1:T(8,128)}, f32[128,128]{0,1:T(8,128)}, f32[128,128]{0,1:T(8,128)}, ...) | async-done | bytes 262160 | tf_op jit(solution)/shard_map/psum | solution.py:99
  (743 shorter events, 578.4 us)
Async XLA Ops:
  7.2 1075.1 %all-reduce.3.cloned.1.call-start = ((), (), s32[]{:S(2)}) async-start(), calls=%async_computation | async-start | bytes 524288 | tf_op jit(solution)/shard_map/psum | solution.py:99
  16.3 8.8 collective-permute-start.2
  38.1 8.8 collective-permute-start.6
  58.5 8.5 collective-permute-start.10
  80.5 8.5 collective-permute-start.14
  100.2 9.9 collective-permute-start.18
  123.3 10.0 collective-permute-start.22
  126.6 7.8 collective-permute-start.23
  147.0 10.0 collective-permute-start.26
  150.3 7.8 collective-permute-start.27
  170.6 32.4 %collective-permute-start.30 = (f32[4,2,130,1]{2,0,3,1:T(4,128)S(1)}, f32[4,2,130,1]{2,0,3,1:T(4,128)S(1)}, u32[]{:S(2)}, u32[]{:S(2)}) collective-permute-start(f32[4,2,130,1]{2,0,3,1:T(4,128)S(1)} %copy.181), channel_id=1, source_target_pairs={{1,0},{2,1},{3,2},{5,4},{6,5},{7,6},{9,8},{10,9},{11,10},{13,12},{... | collective-permute-start | bytes 12488 | tf_op jit(solution)/shard_map/ppermute | solution.py:26
  173.9 30.2 %collective-permute-start.31 = (f32[4,2,130,1]{2,0,3,1:T(4,128)S(1)}, f32[4,2,130,1]{2,0,3,1:T(4,128)S(1)}, u32[]{:S(2)}, u32[]{:S(2)}) collective-permute-start(f32[4,2,130,1]{2,0,3,1:T(4,128)S(1)} %copy.183), channel_id=1, source_target_pairs={{0,1},{1,2},{2,3},{4,5},{5,6},{6,7},{8,9},{9,10},{10,11},{12,13},{... | collective-permute-start | bytes 12488 | tf_op jit(solution)/shard_map/ppermute | solution.py:24
  233.1 12.0 %collective-permute-start.34 = (f32[4,2,130,1]{2,0,3,1:T(4,128)S(1)}, f32[4,2,130,1]{2,0,3,1:T(4,128)S(1)}, u32[]{:S(2)}, u32[]{:S(2)}) collective-permute-start(f32[4,2,130,1]{2,0,3,1:T(4,128)S(1)} %copy.200), channel_id=1, source_target_pairs={{1,0},{2,1},{3,2},{5,4},{6,5},{7,6},{9,8},{10,9},{11,10},{13,12},{... | collective-permute-start | bytes 12488 | tf_op jit(solution)/shard_map/ppermute | solution.py:26
  256.0 8.8 collective-permute-start.38
  275.9 8.8 collective-permute-start.42
  298.2 8.5 collective-permute-start.46
  318.0 9.9 collective-permute-start.50
  341.0 9.9 collective-permute-start.54
  344.3 7.7 collective-permute-start.55
  364.5 9.5 collective-permute-start.58
  387.7 31.6 %collective-permute-start.62 = (f32[4,2,130,1]{2,0,3,1:T(4,128)S(1)}, f32[4,2,130,1]{2,0,3,1:T(4,128)S(1)}, u32[]{:S(2)}, u32[]{:S(2)}) collective-permute-start(f32[4,2,130,1]{2,0,3,1:T(4,128)S(1)} %copy.228), channel_id=1, source_target_pairs={{1,0},{2,1},{3,2},{5,4},{6,5},{7,6},{9,8},{10,9},{11,10},{13,12},{... | collective-permute-start | bytes 12488 | tf_op jit(solution)/shard_map/ppermute | solution.py:26
  391.0 29.4 %collective-permute-start.63 = (f32[4,2,130,1]{2,0,3,1:T(4,128)S(1)}, f32[4,2,130,1]{2,0,3,1:T(4,128)S(1)}, u32[]{:S(2)}, u32[]{:S(2)}) collective-permute-start(f32[4,2,130,1]{2,0,3,1:T(4,128)S(1)} %copy.230), channel_id=1, source_target_pairs={{0,1},{1,2},{2,3},{4,5},{5,6},{6,7},{8,9},{9,10},{10,11},{12,13},{... | collective-permute-start | bytes 12488 | tf_op jit(solution)/shard_map/ppermute | solution.py:24
  451.7 12.7 %collective-permute-start.66 = (f32[4,2,130,1]{2,0,3,1:T(4,128)S(1)}, f32[4,2,130,1]{2,0,3,1:T(4,128)S(1)}, u32[]{:S(2)}, u32[]{:S(2)}) collective-permute-start(f32[4,2,130,1]{2,0,3,1:T(4,128)S(1)} %copy.247), channel_id=1, source_target_pairs={{1,0},{2,1},{3,2},{5,4},{6,5},{7,6},{9,8},{10,9},{11,10},{13,12},{... | collective-permute-start | bytes 12488 | tf_op jit(solution)/shard_map/ppermute | solution.py:26
  478.6 10.3 collective-permute-start.70
  482.5 8.2 collective-permute-start.71
  505.5 9.0 collective-permute-start.74
  528.2 9.5 collective-permute-start.78
  551.8 9.5 collective-permute-start.82
  575.4 9.5 collective-permute-start.86
  599.0 9.5 collective-permute-start.90
  622.8 33.6 %collective-permute-start.94 = (f32[4,2,130,1]{2,0,3,1:T(4,128)S(1)}, f32[4,2,130,1]{2,0,3,1:T(4,128)S(1)}, u32[]{:S(2)}, u32[]{:S(2)}) collective-permute-start(f32[4,2,130,1]{2,0,3,1:T(4,128)S(1)} %copy.279), channel_id=1, source_target_pairs={{1,0},{2,1},{3,2},{5,4},{6,5},{7,6},{9,8},{10,9},{11,10},{13,12},{... | collective-permute-start | bytes 12488 | tf_op jit(solution)/shard_map/ppermute | solution.py:26
  626.1 31.4 %collective-permute-start.95 = (f32[4,2,130,1]{2,0,3,1:T(4,128)S(1)}, f32[4,2,130,1]{2,0,3,1:T(4,128)S(1)}, u32[]{:S(2)}, u32[]{:S(2)}) collective-permute-start(f32[4,2,130,1]{2,0,3,1:T(4,128)S(1)} %copy.281), channel_id=1, source_target_pairs={{0,1},{1,2},{2,3},{4,5},{5,6},{6,7},{8,9},{9,10},{10,11},{12,13},{... | collective-permute-start | bytes 12488 | tf_op jit(solution)/shard_map/ppermute | solution.py:24
  690.0 13.3 %collective-permute-start.98 = (f32[4,2,130,1]{2,0,3,1:T(4,128)}, f32[4,2,130,1]{2,0,3,1:T(4,128)}, u32[]{:S(2)}, u32[]{:S(2)}) collective-permute-start(f32[4,2,130,1]{2,0,3,1:T(4,128)} %copy.309), channel_id=1, source_target_pairs={{1,0},{2,1},{3,2},{5,4},{6,5},{7,6},{9,8},{10,9},{11,10},{13,12},{... | collective-permute-start | bytes 12488 | tf_op jit(solution)/shard_map/ppermute | solution.py:26
  696.8 8.3 collective-permute-start.99
  719.1 9.7 collective-permute-start.102
  744.9 10.1 collective-permute-start.106
  748.8 8.0 collective-permute-start.107
  771.1 9.3 collective-permute-start.110
  796.5 9.7 collective-permute-start.114
  822.3 9.7 collective-permute-start.118
  838.3 30.0 %collective-permute-start.120 = (f32[4,2,1,128]{3,2,0,1:T(1,128)S(1)}, f32[4,2,1,128]{3,2,0,1:T(1,128)S(1)}, u32[]{:S(2)}, u32[]{:S(2)}) collective-permute-start(f32[4,2,1,128]{3,2,0,1:T(1,128)S(1)} %get-tuple-element.150), channel_id=1, source_target_pairs={{4,0},{8,4},{12,8},{5,1},{9,5},{13,9},{6,2},{10,6},{14,10},{7,3},{... | collective-permute-start | bytes 12296 | tf_op jit(solution)/shard_map/ppermute | solution.py:26
  839.6 28.7 %collective-permute-start.121 = (f32[4,2,1,128]{3,2,0,1:T(1,128)S(1)}, f32[4,2,1,128]{3,2,0,1:T(1,128)S(1)}, u32[]{:S(2)}, u32[]{:S(2)}) collective-permute-start(f32[4,2,1,128]{3,2,0,1:T(1,128)S(1)} %get-tuple-element.149), channel_id=1, source_target_pairs={{0,4},{4,8},{8,12},{1,5},{5,9},{9,13},{2,6},{6,10},{10,14},{3,7},{... | collective-permute-start | bytes 12296 | tf_op jit(solution)/shard_map/ppermute | solution.py:24
  871.5 28.6 %collective-permute-start.122 = (f32[4,2,130,1]{2,0,3,1:T(4,128)}, f32[4,2,130,1]{2,0,3,1:T(4,128)}, u32[]{:S(2)}, u32[]{:S(2)}) collective-permute-start(f32[4,2,130,1]{2,0,3,1:T(4,128)} %copy.339), channel_id=1, source_target_pairs={{1,0},{2,1},{3,2},{5,4},{6,5},{7,6},{9,8},{10,9},{11,10},{13,12},{... | collective-permute-start | bytes 12488 | tf_op jit(solution)/shard_map/ppermute | solution.py:26
  878.6 23.3 %collective-permute-start.123 = (f32[4,2,130,1]{2,0,3,1:T(4,128)}, f32[4,2,130,1]{2,0,3,1:T(4,128)}, u32[]{:S(2)}, u32[]{:S(2)}) collective-permute-start(f32[4,2,130,1]{2,0,3,1:T(4,128)} %copy.341), channel_id=1, source_target_pairs={{0,1},{1,2},{2,3},{4,5},{5,6},{6,7},{8,9},{9,10},{10,11},{12,13},{... | collective-permute-start | bytes 12488 | tf_op jit(solution)/shard_map/ppermute | solution.py:24
  907.1 29.1 %collective-permute-start.124 = (f32[4,2,1,128]{3,2,0,1:T(1,128)}, f32[4,2,1,128]{3,2,0,1:T(1,128)S(1)}, u32[]{:S(2)}, u32[]{:S(2)}) collective-permute-start(f32[4,2,1,128]{3,2,0,1:T(1,128)} %get-tuple-element.148), channel_id=1, source_target_pairs={{4,0},{8,4},{12,8},{5,1},{9,5},{13,9},{6,2},{10,6},{14,10},{7,3},{... | collective-permute-start | bytes 12296 | tf_op jit(solution)/shard_map/ppermute | solution.py:26
  908.5 27.7 %collective-permute-start.125 = (f32[4,2,1,128]{3,2,0,1:T(1,128)S(1)}, f32[4,2,1,128]{3,2,0,1:T(1,128)S(1)}, u32[]{:S(2)}, u32[]{:S(2)}) collective-permute-start(f32[4,2,1,128]{3,2,0,1:T(1,128)S(1)} %get-tuple-element.147), channel_id=1, source_target_pairs={{0,4},{4,8},{8,12},{1,5},{5,9},{9,13},{2,6},{6,10},{10,14},{3,7},{... | collective-permute-start | bytes 12296 | tf_op jit(solution)/shard_map/ppermute | solution.py:24
  940.5 34.8 %collective-permute-start.126 = (f32[4,2,130,1]{2,0,3,1:T(4,128)}, f32[4,2,130,1]{2,0,3,1:T(4,128)}, u32[]{:S(2)}, u32[]{:S(2)}) collective-permute-start(f32[4,2,130,1]{2,0,3,1:T(4,128)} %copy.343), channel_id=1, source_target_pairs={{1,0},{2,1},{3,2},{5,4},{6,5},{7,6},{9,8},{10,9},{11,10},{13,12},{... | collective-permute-start | bytes 12488 | tf_op jit(solution)/shard_map/ppermute | solution.py:26
  944.4 31.9 %collective-permute-start.127 = (f32[4,2,130,1]{2,0,3,1:T(4,128)}, f32[4,2,130,1]{2,0,3,1:T(4,128)}, u32[]{:S(2)}, u32[]{:S(2)}) collective-permute-start(f32[4,2,130,1]{2,0,3,1:T(4,128)} %copy.345), channel_id=1, source_target_pairs={{0,1},{1,2},{2,3},{4,5},{5,6},{6,7},{8,9},{9,10},{10,11},{12,13},{... | collective-permute-start | bytes 12488 | tf_op jit(solution)/shard_map/ppermute | solution.py:24
  (189 other events, 2190.4 us)
Sparse Core Ops, SparseCore 0:
  1014.3 67.8 all-reduce.2
where the time goes:
time: 1110 us; the launch traced here: 1090 us
  starting transfers between devices  461 us (42%)
  other arithmetic  234 us (21%)
  local copies, waits for them, and re-layouts  204 us (18%)
  blocking collectives  93.8 us (8%)
  waiting for transfers between devices  81.5 us (7%)
  between operations  17.7 us (2%)
    ppermute x64, starting transfers between devices, with_halo(): lax.ppermute(tail, axis, [(i, (i + 1) % count) for i in range(ends)])  343 us
    ppermute x64, starting transfers between devices, with_halo(): lax.ppermute(head, axis, [((i + 1) % count, i) for i in range(ends)])  118 us
    all_gather x4, blocking collectives, per_device(): slowness_tile = lax.all_gather(velocity[depth], 'freq', axis=0, tiled=True)  93.8 us
    reduce_sum x4, other arithmetic, per_device(): partial_image = jnp.sum(real_part, axis=0)  78.8 us
    slice x64, local copies, waits for them, and re-layouts, with_halo(): head = lax.slice_in_dim(cells, 0, width, axis=dim)  76.7 us
    concatenate x64, other arithmetic, with_halo(): jnp.concatenate([lax.ppermute(tail, axis, [(i, (i + 1) % count) for i in...  58.1 us
    psum x1, waiting for transfers between devices, per_device(): image_rows.append(lax.psum(partial_image, 'freq') / math.sqrt(freq_total))  56.6 us
    slice x61, local copies, waits for them, and re-layouts, with_halo(): lax.slice_in_dim(cells, cells.shape[dim] - width, cells.shape[dim], axis=...  42.8 us
  transfers between devices with their start and end apart: 129, of which 38 were waited for; matrix products, arithmetic and copies ran while one was open for 14% of the time, Pallas kernels for 0%

commit v1 on v0

v1 whole, which is shorter than its diff:
```python
import functools
import math

import jax
import jax.numpy as jnp
from jax import lax
from jax.experimental import pallas as pl
from jax.experimental.pallas import tpu as pltpu
from jax.sharding import PartitionSpec as P

ORDER = 8
LOWEST = 2.0
HIGHEST = 60.0
INTERVAL = 0.01
MESH = pl.DeviceIdType.MESH

SPAN = 2
LANE_BLOCKS = 16
SUB_BLOCKS = 8


def term_weights(order):
    values = [1.0 / (term + 1) for term in range(order + 1)]
    whole = sum(values)
    return [value / whole for value in values]


def kernel(
    dims,
    wave_hbm, vel_hbm, image_hbm, out_hbm,
    terms, pair_sum, quarter, slow, rows_buf, tile, edge_r, edge_l, halo_l, halo_r, natural,
    vel_tile, vel_edge_r, vel_edge_l, vel_halo_l, vel_halo_r,
    part_image, image_in, image_out,
    load_sem, wave_send, wave_recv, vel_send, vel_recv, velh_send, velh_recv,
    red_send, red_recv, cast_send, cast_recv, store_sem,
):
    depths, span, freqs, side, fcount, xcount, ycount = dims
    order = ORDER
    weights = term_weights(order)
    reach = order * span
    extent = side + 2 * reach
    nx = extent // LANE_BLOCKS
    ny = extent // SUB_BLOCKS
    slab_rows = nx * 8
    batch = 2 * freqs
    inner = min(batch, 128 // reach)
    groups = batch // inner
    strip = side // fcount
    rounds = depths // span

    me_f = lax.axis_index("freq")
    me_x = lax.axis_index("gx")
    me_y = lax.axis_index("gy")

    def mod(value, count):
        return lax.rem(value + count, count)

    up, down = mod(me_x - 1, xcount), mod(me_x + 1, xcount)
    left, right = mod(me_y - 1, ycount), mod(me_y + 1, ycount)
    around = [
        {"gx": up, "gy": me_y}, {"gx": down, "gy": me_y}, {"gx": me_x, "gy": right}, {"gx": me_x, "gy": left},
        {"gx": up, "gy": right}, {"gx": down, "gy": right}, {"gx": up, "gy": left}, {"gx": down, "gy": left},
    ]
    peers = [mod(me_f + k, fcount) for k in range(1, fcount)]

    loads = []
    for f in range(freqs):
        for part in range(2):
            loads.append(
                pltpu.make_async_copy(
                    wave_hbm.at[f, part], tile.at[0, part * freqs + f, pl.ds(reach, side)], load_sem.at[f * 2 + part]
                )
            )
    own_rows = pl.multiple_of(reach + me_f * strip, 8)
    vel_load = pltpu.make_async_copy(vel_hbm, vel_tile.at[:, pl.ds(own_rows, strip)], load_sem.at[batch])
    for copy in loads:
        copy.start()
    vel_load.start()

    barrier = pltpu.get_barrier_semaphore()
    for device in around:
        pl.semaphore_signal(barrier, inc=1, device_id=device, device_id_type=MESH)
    for peer in peers:
        pl.semaphore_signal(barrier, inc=1, device_id={"freq": peer}, device_id_type=MESH)

    lane = lax.broadcasted_iota(jnp.int32, (1, 128), 1)
    for copy in loads:
        copy.wait()
    vel_load.wait()

    def build_edges(r):
        def place(source, columns_end):
            for g in range(groups):
                made = None
                for k in range(inner):
                    cells = source(k * groups + g)
                    shift = (k * reach - columns_end) % 128
                    moved = cells if shift == 0 else pltpu.roll(cells, shift, 1)
                    made = moved if made is None else jnp.where(lane >= k * reach, moved, made)
                yield g, made

        def step(i, _):
            rows = pl.ds(pl.multiple_of(i * 32, 32), 32)
            source_rows = pl.ds(pl.multiple_of(reach + i * 32, 8), 32)
            for g, made in place(lambda b: tile[r, b, source_rows, :], side - reach):
                edge_r[r, g, rows, :] = made
            for g, made in place(lambda b: tile[r, b, source_rows, :], 0):
                edge_l[r, g, rows, :] = made
            return 0

        lax.fori_loop(0, side // 32, step, 0)

    def wave_copies(r):
        head, tail = pl.ds(0, reach), pl.ds(side - reach, reach)
        low, mid, high = pl.ds(0, reach), pl.ds(reach, side), pl.ds(reach + side, reach)
        own_head, own_tail = pl.ds(reach, reach), pl.ds(side, reach)
        pairs = [
            (tile.at[r, :, own_head], tile.at[r, :, high]),
            (tile.at[r, :, own_tail], tile.at[r, :, low]),
            (edge_r.at[r], halo_l.at[r, :, mid]),
            (edge_l.at[r], halo_r.at[r, :, mid]),
            (edge_r.at[r, :, head], halo_l.at[r, :, high]),
            (edge_r.at[r, :, tail], halo_l.at[r, :, low]),
            (edge_l.at[r, :, head], halo_r.at[r, :, high]),
            (edge_l.at[r, :, tail], halo_r.at[r, :, low]),
        ]
        return [
            pltpu.make_async_remote_copy(
                src_ref=source, dst_ref=target, send_sem=wave_send.at[r, k], recv_sem=wave_recv.at[r, k],
                device_id=around[k], device_id_type=MESH,
            )
            for k, (source, target) in enumerate(pairs)
        ]

    def vel_copies():
        return [
            pltpu.make_async_remote_copy(
                src_ref=vel_tile.at[:, pl.ds(own_rows, strip)], dst_ref=vel_tile.at[:, pl.ds(own_rows, strip)],
                send_sem=vel_send.at[k], recv_sem=vel_recv.at[k],
                device_id={"freq": peer}, device_id_type=MESH,
            )
            for k, peer in enumerate(peers)
        ]

    def vel_halo_copies():
        head, tail = pl.ds(0, reach), pl.ds(side - reach, reach)
        low, mid, high = pl.ds(0, reach), pl.ds(reach, side), pl.ds(reach + side, reach)
        own_head, own_tail = pl.ds(reach, reach), pl.ds(side, reach)
        pairs = [
            (vel_tile.at[:, own_head], vel_tile.at[:, high]),
            (vel_tile.at[:, own_tail], vel_tile.at[:, low]),
            (vel_edge_r, vel_halo_l.at[mid]),
            (vel_edge_l, vel_halo_r.at[mid]),
            (vel_edge_r.at[head], vel_halo_l.at[high]),
            (vel_edge_r.at[tail], vel_halo_l.at[low]),
            (vel_edge_l.at[head], vel_halo_r.at[high]),
            (vel_edge_l.at[tail], vel_halo_r.at[low]),
        ]
        return [
            pltpu.make_async_remote_copy(
                src_ref=source, dst_ref=target, send_sem=velh_send.at[k], recv_sem=velh_recv.at[k],
                device_id=around[k], device_id_type=MESH,
            )
            for k, (source, target) in enumerate(pairs)
        ]

    build_edges(0)
    pl.semaphore_wait(barrier, len(around) + len(peers))
    first_wave = wave_copies(0)
    for copy in first_wave:
        copy.start()
    vel_sends = vel_copies()
    for copy in vel_sends:
        copy.start()

    lanes8 = lax.broadcasted_iota(jnp.int32, (8, 128), 1)
    subs8 = lax.broadcasted_iota(jnp.int32, (8, 128), 0)
    x_base = me_x * side - reach + lax.rem(lanes8, LANE_BLOCKS) * nx
    y_base = me_y * side - reach + subs8 * ny

    def fill_quarter(yi, _):
        inside_y = jnp.where((y_base + yi >= 0) & (y_base + yi < ycount * side), 0.25, 0.0)
        for xi in range(nx):
            inside = jnp.where((x_base + xi >= 0) & (x_base + xi < xcount * side), inside_y, 0.0)
            quarter[pl.ds(pl.multiple_of(yi * slab_rows + xi * 8, 8), 8), :] = inside
        return 0

    lax.fori_loop(0, ny, fill_quarter, 0)

    per_step = 4 if nx % 4 == 0 else (3 if nx % 3 == 0 else 2)

    def gather_blocks(load):
        pieces = []
        for half in range(LANE_BLOCKS // 8):
            pieces.append(load(half * 8 * nx))
        return pieces

    def assemble_wave(r):
        def some(i, _):
            for j in range(per_step):
                xi = i * per_step + j
                pieces = []
                for b in range(batch):
                    pieces += gather_blocks(lambda start: tile[r, b, pl.ds(xi + start, 8, stride=nx), :])
                rows_buf[xi, pl.ds(reach, side), :] = jnp.concatenate(pieces, axis=0).T
                from_l, from_r = [], []
                for g in range(groups):
                    from_l += gather_blocks(lambda start: halo_l[r, g, pl.ds(xi + start, 8, stride=nx), :])
                    from_r += gather_blocks(lambda start: halo_r[r, g, pl.ds(xi + start, 8, stride=nx), :])
                from_l, from_r = jnp.concatenate(from_l, axis=0), jnp.concatenate(from_r, axis=0)
                pieces = []
                for k in range(inner):
                    moved_l = from_l if k == 0 else pltpu.roll(from_l, 128 - k * reach, 1)
                    shift = (reach - k * reach) % 128
                    moved_r = from_r if shift == 0 else pltpu.roll(from_r, shift, 1)
                    pieces.append(jnp.where(lane < reach, moved_l, moved_r))
                beside = jnp.concatenate(pieces, axis=0).T
                rows_buf[xi, pl.ds(0, reach), :] = beside[:reach]
                rows_buf[xi, pl.ds(reach + side, reach), :] = beside[reach : 2 * reach]
            return 0

        lax.fori_loop(0, nx // per_step, some, 0)

        def pack(xi, _):
            for yi in range(ny):
                rows = pl.ds(pl.multiple_of(yi * slab_rows + xi * 8, 8), 8)
                terms[0, rows, :] = rows_buf[xi, pl.ds(yi, 8, stride=ny), :] * (quarter[rows, :] * 4.0)
            return 0

        lax.fori_loop(0, nx, pack, 0)

    with_vel_halo = span > 1

    def assemble_vel(d):
        def some(i, _):
            for j in range(per_step):
                xi = i * per_step + j
                pieces = gather_blocks(lambda start: vel_tile[d, pl.ds(xi + start, 8, stride=nx), :])
                rows_buf[xi, pl.ds(reach, side), :] = jnp.concatenate(pieces * batch, axis=0).T
                if with_vel_halo:
                    from_l = jnp.concatenate(gather_blocks(lambda start: vel_halo_l[pl.ds(xi + start, 8, stride=nx), :]), axis=0)
                    from_r = jnp.concatenate(gather_blocks(lambda start: vel_halo_r[pl.ds(xi + start, 8, stride=nx), :]), axis=0)
                    shift_l = (-(32 * d + 32 - reach)) % 128
                    shift_r = (reach - 32 * d) % 128
                    moved_l = from_l if shift_l == 0 else pltpu.roll(from_l, shift_l, 1)
                    moved_r = from_r if shift_r == 0 else pltpu.roll(from_r, shift_r, 1)
                    both = jnp.where(lane < reach, moved_l, moved_r)
                    beside = jnp.concatenate([both] * batch, axis=0).T
                    rows_buf[xi, pl.ds(0, reach), :] = beside[:reach]
                    rows_buf[xi, pl.ds(reach + side, reach), :] = beside[reach : 2 * reach]
                else:
                    rows_buf[xi, pl.ds(0, reach), :] = jnp.ones((reach, 128), jnp.float32)
                    rows_buf[xi, pl.ds(reach + side, reach), :] = jnp.ones((reach, 128), jnp.float32)
            return 0

        lax.fori_loop(0, nx // per_step, some, 0)

        def pack(xi, _):
            for yi in range(ny):
                rows = pl.ds(pl.multiple_of(yi * slab_rows + xi * 8, 8), 8)
                slow[d, rows, :] = (INTERVAL / (order + 1)) / rows_buf[xi, pl.ds(yi, 8, stride=ny), :]
            return 0

        lax.fori_loop(0, nx, pack, 0)

    def slab(n, yi):
        return terms[n, pl.ds(yi * slab_rows, slab_rows), :].reshape(nx, 8, 128)

    def x_sum(cells):
        before = pltpu.roll(cells[nx - 1 : nx], 1, 2)
        after = pltpu.roll(cells[0:1], 127, 2)
        wide = jnp.concatenate([before, cells, after], axis=0)
        twos = wide[:-1] + wide[1:]
        return twos[:-1] + twos[1:]

    def next_term(n, first):
        here = slab(n, 0)
        sum_here = x_sum(here)
        sum_first = sum_here
        twos = pltpu.roll(x_sum(slab(n, ny - 1)), 1, 1) + sum_here
        for yi in range(ny):
            if yi + 1 < ny:
                after = slab(n, yi + 1)
                sum_after = x_sum(after)
            else:
                after = None
                sum_after = pltpu.roll(sum_first, 7, 1)
            twos_after = sum_here + sum_after
            nine = twos + twos_after
            rows = pl.ds(yi * slab_rows, slab_rows)
            scale = quarter[rows, :].reshape(nx, 8, 128)
            if first:
                pair = (0.5 * scale) * nine
            else:
                pair = scale * nine - pair_sum[rows, :].reshape(nx, 8, 128)
            pair_sum[rows, :] = pair.reshape(slab_rows, 128)
            terms[n + 1, rows, :] = (pair - here).reshape(slab_rows, 128)
            twos, sum_here, here = twos_after, sum_after, after

    def all_terms():
        next_term(0, True)

        def body(n, _):
            next_term(n, False)
            return 0

        lax.fori_loop(1, order, body, 0)

    frequency = me_f * freqs + lax.rem(lanes8 // LANE_BLOCKS, freqs)
    omega = (2.0 * math.pi) * (
        LOWEST + (HIGHEST - LOWEST) * (frequency.astype(jnp.float32) + 0.5) / (freqs * fcount)
    )
    sign = jnp.where(lanes8 < 64, -1.0, 1.0)

    vregs = nx * ny
    chunk = max(c for c in range(8, 37) if vregs % c == 0)

    def phase_sum(d):
        def body(i, _):
            rows = pl.ds(pl.multiple_of(i * chunk * 8, 8), chunk * 8)

            def term(n):
                return terms[n, rows, :].reshape(chunk, 8, 128)

            angle = omega * slow[d, rows, :].reshape(chunk, 8, 128)
            square = angle * angle
            cosine = 1.0 + square * (-0.5 + square * (1 / 24.0 + square * (-1 / 720.0 + square * (1 / 40320.0))))
            sine = angle * (sign * (1.0 + square * (-1 / 6.0 + square * (1 / 120.0 + square * (-1 / 5040.0)))))
            double = cosine + cosine
            later = weights[order] * term(order)
            now = weights[order - 1] * term(order - 1) + double * later
            for n in range(order - 2, -1, -1):
                now, later = weights[n] * term(n) + double * now - later, now
            new = cosine * now + sine * pltpu.roll(now, 64, 2) - later
            terms[0, rows, :] = new.reshape(chunk * 8, 128)
            return 0

        lax.fori_loop(0, vregs // chunk, body, 0)

    def to_natural(d, whole):
        def unpack(xi, _):
            for yi in range(ny):
                rows = pl.ds(pl.multiple_of(yi * slab_rows + xi * 8, 8), 8)
                rows_buf[xi, pl.ds(yi, 8, stride=ny), :] = terms[0, rows, :]
            return 0

        lax.fori_loop(0, nx, unpack, 0)

        def some(i, _):
            for j in range(per_step):
                xi = i * per_step + j
                turned = rows_buf[xi, pl.ds(reach, side), :].T
                for half in range(LANE_BLOCKS // 8):
                    target = pl.ds(xi + half * 8 * nx, 8, stride=nx)
                    blocks = [turned[b * 16 + half * 8 : b * 16 + half * 8 + 8] for b in range(batch)]
                    if whole:
                        for b in range(batch):
                            natural[b, target, :] = blocks[b]
                    total = blocks[0]
                    for b in range(1, freqs):
                        total = total + blocks[b]
                    part_image[d, target, :] = total
            return 0

        lax.fori_loop(0, nx // per_step, some, 0)

    def reduce_copies(d):
        return [
            pltpu.make_async_remote_copy(
                src_ref=part_image.at[d, pl.ds(pl.multiple_of(reach + peer * strip, 8), strip)],
                dst_ref=image_in.at[d, k],
                send_sem=red_send.at[d, k], recv_sem=red_recv.at[d, k],
                device_id={"freq": peer}, device_id_type=MESH,
            )
            for k, peer in enumerate(peers)
        ]

    image_rows = pl.ds(pl.multiple_of(me_f * strip, 8), strip)

    def cast_copies(d):
        return [
            pltpu.make_async_remote_copy(
                src_ref=image_out.at[d, image_rows], dst_ref=image_out.at[d, image_rows],
                send_sem=cast_send.at[d, k], recv_sem=cast_recv.at[d, k],
                device_id={"freq": peer}, device_id_type=MESH,
            )
            for k, peer in enumerate(peers)
        ]

    sent_images = {}

    def send_image(d):
        sent_images[d] = reduce_copies(d)
        for copy in sent_images[d]:
            copy.start()

    def finish_image(d):
        for copy in sent_images[d]:
            copy.wait()
        total = part_image[d, pl.ds(own_rows, strip), :]
        for k in range(fcount - 1):
            total = total + image_in[d, k]
        image_out[d, image_rows, :] = total * (1.0 / math.sqrt(freqs * fcount))
        casts = cast_copies(d)
        for copy in casts:
            copy.start()
        return casts

    casts = []
    for r in range(rounds):
        if r == 0:
            copies = first_wave
            for copy in vel_sends:
                copy.wait()
            if with_vel_halo:
                for source, target in ((96, vel_edge_r), (0, vel_edge_l)):
                    made = None
                    for d in range(depths):
                        cells = vel_tile[d, pl.ds(reach, side), :]
                        shift = (32 * d - source) % 128
                        moved = cells if shift == 0 else pltpu.roll(cells, shift, 1)
                        made = moved if made is None else jnp.where(lane >= 32 * d, moved, made)
                    target[...] = made
                vel_sends = vel_halo_copies()
                for copy in vel_sends:
                    copy.start()
            else:
                for d in range(depths):
                    vel_tile[d, pl.ds(0, reach), :] = jnp.ones((reach, side), jnp.float32)
                    vel_tile[d, pl.ds(reach + side, reach), :] = jnp.ones((reach, side), jnp.float32)
        else:
            for b in range(batch):
                tile[r, b, pl.ds(reach, side), :] = natural[b, pl.ds(reach, side), :]
            build_edges(r)
            copies = wave_copies(r)
            for copy in copies:
                copy.start()
        if r == 0 and not with_vel_halo:
            for d in range(depths):
                assemble_vel(d)
        for copy in copies:
            copy.wait()
        assemble_wave(r)
        for step in range(span):
            d = r * span + step
            all_terms()
            if d == 0 and with_vel_halo:
                for copy in vel_sends:
                    copy.wait()
                for e in range(depths):
                    assemble_vel(e)
            if d > 0:
                casts += finish_image(d - 1)
            phase_sum(d)
            to_natural(d, step == span - 1)
            send_image(d)
    stores = []
    for f in range(freqs):
        for part in range(2):
            stores.append(
                pltpu.make_async_copy(
                    natural.at[part * freqs + f, pl.ds(reach, side)], out_hbm.at[f, part], store_sem.at[f * 2 + part]
                )
            )
    for copy in stores:
        copy.start()
    casts += finish_image(depths - 1)
    for copy in casts:
        copy.wait()
    last = pltpu.make_async_copy(image_out, image_hbm, store_sem.at[batch])
    last.start()
    for copy in stores:
        copy.wait()
    last.wait()


def per_device(wavefield, velocity):
    freqs, _, side, _ = wavefield.shape
    depths = velocity.shape[0]
    fcount, xcount, ycount = lax.axis_size("freq"), lax.axis_size("gx"), lax.axis_size("gy")
    span = SPAN
    rounds = depths // span
    reach = ORDER * span
    extent = side + 2 * reach
    nx, ny = extent // LANE_BLOCKS, extent // SUB_BLOCKS
    cells = nx * ny * 8
    batch = 2 * freqs
    inner = min(batch, 128 // reach)
    groups = batch // inner
    strip = side // fcount
    dims = (depths, span, freqs, side, fcount, xcount, ycount)
    f32 = jnp.float32
    dma = pltpu.SemaphoreType.DMA
    image, extrapolated = pl.pallas_call(
        functools.partial(kernel, dims),
        out_shape=(
            jax.ShapeDtypeStruct((depths, side, side), f32),
            jax.ShapeDtypeStruct(wavefield.shape, f32),
        ),
        in_specs=[pl.BlockSpec(memory_space=pl.ANY)] * 2,
        out_specs=(pl.BlockSpec(memory_space=pl.ANY),) * 2,
        scratch_shapes=[
            pltpu.VMEM((ORDER + 1, cells, 128), f32),
            pltpu.VMEM((cells, 128), f32),
            pltpu.VMEM((cells, 128), f32),
            pltpu.VMEM((depths, cells, 128), f32),
            pltpu.VMEM((nx, extent, 128), f32),
            pltpu.VMEM((rounds, batch, extent, 128), f32),
            pltpu.VMEM((rounds, groups, side, 128), f32),
            pltpu.VMEM((rounds, groups, side, 128), f32),
            pltpu.VMEM((rounds, groups, extent, 128), f32),
            pltpu.VMEM((rounds, groups, extent, 128), f32),
            pltpu.VMEM((batch, extent, 128), f32),
            pltpu.VMEM((depths, extent, 128), f32),
            pltpu.VMEM((side, 128), f32),
            pltpu.VMEM((side, 128), f32),
            pltpu.VMEM((extent, 128), f32),
            pltpu.VMEM((extent, 128), f32),
            pltpu.VMEM((depths, extent, 128), f32),
            pltpu.VMEM((depths, fcount - 1, strip, 128), f32),
            pltpu.VMEM((depths, side, 128), f32),
            dma((batch + 1,)),
            dma((rounds, 8)),
            dma((rounds, 8)),
            dma((fcount - 1,)),
            dma((fcount - 1,)),
            dma((8,)),
            dma((8,)),
            dma((depths, fcount - 1)),
            dma((depths, fcount - 1)),
            dma((depths, fcount - 1)),
            dma((depths, fcount - 1)),
            dma((batch + 1,)),
        ],
        compiler_params=pltpu.CompilerParams(
            collective_id=0, has_side_effects=True, vmem_limit_bytes=56 * 1024 * 1024
        ),
    )(wavefield, velocity)
    return (image, extrapolated)


def solution(mesh):
    placed = (P("freq", None, "gx", "gy"), P(None, ("gx", "freq"), "gy"))
    return jax.shard_map(
        per_device,
        mesh=mesh,
        in_specs=placed,
        out_specs=(P(None, "gx", "gy"), P("freq", None, "gx", "gy")),
        check_vma=False,
    )
```

time: 1110 us -> 65.8 us (0.06)
  the two profiles are of different devices: /device:TPU:1 before, /device:TPU:0 now
where the time goes in v1:
time: 65.8 us; the launch traced here: 65.7 us
  Pallas kernels  62.5 us (95%)
  local copies, waits for them, and re-layouts  2.52 us (4%)
    pallas_call x1, Pallas kernels, per_device(): pl.pallas_call(functools.partial(kernel, dims), out_shape=(jax.ShapeDtype...  62.5 us
    unnamed x4, local copies, waits for them, and re-layouts  2.52 us

profile of v1, /device:TPU:0, one launch (start us, length us, event | category | flops | bytes accessed | tf_op | source)
XLA Modules:
  0.0 65.7 jit_solution(16935193842306505083)
XLA Ops:
  0.6 62.5 %shard_map.41 = (f32[4,128,128]{2,1,0:T(8,128)}, f32[4,2,128,128]{3,2,1,0:T(8,128)}) custom-call(f32[4,2,128,128]{3,2,1,0:T(8,128)} %wave_hbm.1, f32[4,16,128]{2,1,0:T(8,128)} %vel_hbm.1), custom_call_target="tpu_custom_call" | custom-call | tf_op jit(solution)/shard_map/pallas_call | solution.py:494
  63.1 0.0 copy-start
  63.1 1.7 %copy.6 = f32[4,128,128]{2,1,0:T(8,128)} copy(f32[4,128,128]{2,1,0:T(8,128)} %get-tuple-element.4) | data formatting | bytes 524288
  64.9 0.0 copy-done
  64.9 0.8 %copy.7 = f32[4,2,128,128]{3,2,1,0:T(8,128)} copy(f32[4,2,128,128]{3,2,1,0:T(8,128)S(1)} %copy-done) | data formatting | bytes 1048576
Async XLA Ops:
  63.1 1.7 %copy-start = (f32[4,2,128,128]{3,2,1,0:T(8,128)S(1)}, f32[4,2,128,128]{3,2,1,0:T(8,128)}, u32[]{:S(2)}) copy-start(f32[4,2,128,128]{3,2,1,0:T(8,128)} %get-tuple-element.5) | copy-start | bytes 1572868

commit v2 on v0

v2 whole, which is shorter than its diff:
```python
import functools
import math

import jax
import jax.numpy as jnp
from jax import lax
from jax.experimental import pallas as pl
from jax.experimental.pallas import tpu as pltpu
from jax.sharding import PartitionSpec as P

ORDER = 8
LOWEST = 2.0
HIGHEST = 60.0
INTERVAL = 0.01
MESH = pl.DeviceIdType.MESH
SUB_BLOCKS = 8


def ratios(order):
    return [1.0 / (term + 1) for term in range(order + 1)]


def shared_weight(order):
    return 1.0 / sum(1.0 / (term + 1) for term in range(order + 1))


def rolled(cells, shift, axis):
    shift = shift % cells.shape[axis]
    return cells if shift == 0 else pltpu.roll(cells, shift, axis)


def kernel(
    dims,
    wave_hbm, vel_hbm, image_hbm, out_hbm,
    terms, pair_sum, quarter, rows_buf, slow_rows, tile, edge_r, edge_l, halo_l, halo_r, natural,
    vel_raw, slow_tile, slow_edge_r, slow_edge_l, slow_halo_l, slow_halo_r,
    part_image, image_in, image_out,
    load_sem, wave_send, wave_recv, vel_send, vel_recv, velh_send, velh_recv,
    red_send, red_recv, cast_send, cast_recv, store_sem,
):
    depths, freqs, side, fcount, xcount, ycount = dims
    order = ORDER
    weights = ratios(order)
    reach = order * depths
    extent = side + 2 * reach
    lane_blocks = 128 // freqs
    octets = lane_blocks // 8
    nx = extent // lane_blocks
    slab_rows = 2 * nx * 8
    batch = 2 * freqs
    inner = 128 // reach
    groups = batch // inner
    strip = side // fcount
    around_y = [reach - order * d for d in range(depths)]
    blocks_y = [(side + 2 * h) // SUB_BLOCKS for h in around_y]

    me_f = lax.axis_index("freq")
    me_x = lax.axis_index("gx")
    me_y = lax.axis_index("gy")

    def mod(value, count):
        return lax.rem(value + count, count)

    up, down = mod(me_x - 1, xcount), mod(me_x + 1, xcount)
    left, right = mod(me_y - 1, ycount), mod(me_y + 1, ycount)
    around = [
        {"gx": up, "gy": me_y}, {"gx": down, "gy": me_y}, {"gx": me_x, "gy": right}, {"gx": me_x, "gy": left},
        {"gx": up, "gy": right}, {"gx": down, "gy": right}, {"gx": up, "gy": left}, {"gx": down, "gy": left},
    ]
    peers = [mod(me_f + k, fcount) for k in range(1, fcount)]

    barrier = pltpu.get_barrier_semaphore()
    for device in around:
        pl.semaphore_signal(barrier, inc=1, device_id=device, device_id_type=MESH)
    for peer in peers:
        pl.semaphore_signal(barrier, inc=1, device_id={"freq": peer}, device_id_type=MESH)

    vel_load = pltpu.make_async_copy(vel_hbm, vel_raw, load_sem.at[batch])
    vel_load.start()
    loads = []
    for f in range(freqs):
        for part in range(2):
            loads.append(
                pltpu.make_async_copy(
                    wave_hbm.at[f, part], tile.at[part * freqs + f, pl.ds(reach, side)], load_sem.at[f * 2 + part]
                )
            )
    for copy in loads:
        copy.start()

    own_rows = pl.ds(pl.multiple_of(reach + me_f * strip, 8), strip)
    vel_load.wait()
    slow_tile[:, own_rows, :] = (INTERVAL / (order + 1)) / vel_raw[...]
    for copy in loads:
        copy.wait()

    lane = lax.broadcasted_iota(jnp.int32, (1, 128), 1)

    def build_edges(i, _):
        rows = pl.ds(pl.multiple_of(i * 32, 32), 32)
        source_rows = pl.ds(pl.multiple_of(reach + i * 32, 8), 32)
        for target, first in ((edge_r, side - reach), (edge_l, 0)):
            for g in range(groups):
                made = None
                for k in range(inner):
                    moved = rolled(tile[k * groups + g, source_rows, :], k * reach - first, 1)
                    made = moved if made is None else jnp.where(lane >= k * reach, moved, made)
                target[g, rows, :] = made
        return 0

    lax.fori_loop(0, side // 32, build_edges, 0)

    head, tail = pl.ds(0, reach), pl.ds(side - reach, reach)
    low, mid, high = pl.ds(0, reach), pl.ds(reach, side), pl.ds(reach + side, reach)
    own_head, own_tail = pl.ds(reach, reach), pl.ds(side, reach)

    def to_neighbours(pairs, send_sem, recv_sem):
        return [
            pltpu.make_async_remote_copy(
                src_ref=source, dst_ref=target, send_sem=send_sem.at[k], recv_sem=recv_sem.at[k],
                device_id=around[k], device_id_type=MESH,
            )
            for k, (source, target) in enumerate(pairs)
        ]

    def to_peers(pairs, send_sem, recv_sem):
        return [
            pltpu.make_async_remote_copy(
                src_ref=source, dst_ref=target, send_sem=send_sem.at[k], recv_sem=recv_sem.at[k],
                device_id={"freq": peers[k]}, device_id_type=MESH,
            )
            for k, (source, target) in enumerate(pairs)
        ]

    def start(copies):
        for copy in copies:
            copy.start()
        return copies

    def wait(copies):
        for copy in copies:
            copy.wait()

    wave_copies = to_neighbours(
        [
            (tile.at[:, own_head], tile.at[:, high]),
            (tile.at[:, own_tail], tile.at[:, low]),
            (edge_r, halo_l.at[:, mid]),
            (edge_l, halo_r.at[:, mid]),
            (edge_r.at[:, head], halo_l.at[:, high]),
            (edge_r.at[:, tail], halo_l.at[:, low]),
            (edge_l.at[:, head], halo_r.at[:, high]),
            (edge_l.at[:, tail], halo_r.at[:, low]),
        ],
        wave_send, wave_recv,
    )
    stages = [(0, 1), (1, depths - 1)]

    def slow_peer_copies(stage):
        first, count = stages[stage]
        block = slow_tile.at[pl.ds(first, count), own_rows]
        return to_peers([(block, block)] * (fcount - 1), vel_send.at[stage], vel_recv.at[stage])

    def slow_halo_copies(stage):
        first, count = stages[stage]
        of = pl.ds(first, count)
        return to_neighbours(
            [
                (slow_tile.at[of, own_head], slow_tile.at[of, high]),
                (slow_tile.at[of, own_tail], slow_tile.at[of, low]),
                (slow_edge_r.at[stage], slow_halo_l.at[stage, mid]),
                (slow_edge_l.at[stage], slow_halo_r.at[stage, mid]),
                (slow_edge_r.at[stage, head], slow_halo_l.at[stage, high]),
                (slow_edge_r.at[stage, tail], slow_halo_l.at[stage, low]),
                (slow_edge_l.at[stage, head], slow_halo_r.at[stage, high]),
                (slow_edge_l.at[stage, tail], slow_halo_r.at[stage, low]),
            ],
            velh_send.at[stage], velh_recv.at[stage],
        )

    def build_slow_edges(stage):
        first, count = stages[stage]
        for target, source in ((slow_edge_r, side - reach), (slow_edge_l, 0)):
            made = None
            for j in range(count):
                moved = rolled(slow_tile[first + j, pl.ds(reach, side), :], reach * j - source, 1)
                made = moved if made is None else jnp.where(lane >= reach * j, moved, made)
            target[stage] = made

    pl.semaphore_wait(barrier, len(around) + len(peers))
    slow_first = start(slow_peer_copies(0))
    start(wave_copies)
    slow_rest = start(slow_peer_copies(1))

    lanes8 = lax.broadcasted_iota(jnp.int32, (8, 128), 1)
    subs8 = lax.broadcasted_iota(jnp.int32, (8, 128), 0)

    def inside_x(xi, lanes):
        x = me_x * side - reach + lax.rem(lanes, lane_blocks) * nx + xi
        return (x >= 0) & (x < xcount * side)

    for d in range(depths):
        def fill_quarter(yi, _):
            y = me_y * side - around_y[d] + subs8 * blocks_y[d] + yi
            inside_y = jnp.where((y >= 0) & (y < ycount * side), 0.25, 0.0)
            for xi in range(nx):
                rows = pl.ds(pl.multiple_of((yi * nx + xi) * 8, 8), 8)
                quarter[d, rows, :] = jnp.where(inside_x(xi, lanes8), inside_y, 0.0)
            return 0

        lax.fori_loop(0, blocks_y[d], fill_quarter, 0)

    def blocks_of(load):
        return jnp.concatenate([load(8 * nx * o) for o in range(octets)], axis=0)

    def place_slow_tile(d):
        for xi in range(nx):
            cells = blocks_of(lambda begin: slow_tile[d, pl.ds(xi + begin, 8, stride=nx), :])
            slow_rows[d, xi, pl.ds(around_y[d], side), :] = jnp.concatenate([cells] * freqs, axis=0).T

    def place_slow_halo(stage):
        first, count = stages[stage]
        for pair in range(0, count, 2):
            for xi in range(nx):
                from_l = blocks_of(lambda begin: slow_halo_l[stage, pl.ds(xi + begin, 8, stride=nx), :])
                from_r = blocks_of(lambda begin: slow_halo_r[stage, pl.ds(xi + begin, 8, stride=nx), :])
                made = jnp.where(lane < reach, rolled(from_l, -reach * pair, 1), rolled(from_r, reach - reach * pair, 1))
                if pair + 1 < count:
                    made = jnp.where(lane < 2 * reach, made, rolled(from_l, reach * (1 - pair), 1))
                    made = jnp.where(lane < 3 * reach, made, rolled(from_r, reach * (2 - pair), 1))
                turned = jnp.concatenate([made] * freqs, axis=0).T
                for j in range(min(2, count - pair)):
                    d = first + pair + j
                    h = around_y[d]
                    base = 2 * reach * j
                    slow_rows[d, xi, pl.ds(0, h), :] = turned[base + reach - h : base + reach]
                    slow_rows[d, xi, pl.ds(h + side, h), :] = turned[base + reach : base + reach + h]

    def assemble_wave():
        ny = blocks_y[0]
        inside_l = jnp.where(me_y > 0, 1.0, 0.0)
        inside_r = jnp.where(me_y < ycount - 1, 1.0, 0.0)

        def put(part, xi, y0, block):
            yb, yi = y0 // ny, y0 % ny
            begin = ((yi * 2 + part) * nx + xi) * 8 + yb
            terms[0, pl.ds(begin, 8, stride=slab_rows), :] = block

        def some(xi, _):
            grid_x = jnp.where(inside_x(xi, lane), 1.0, 0.0)
            for part in range(2):
                cells = jnp.concatenate(
                    [
                        blocks_of(lambda begin: tile[part * freqs + f, pl.ds(xi + begin, 8, stride=nx), :])
                        for f in range(freqs)
                    ],
                    axis=0,
                )
                turned = cells.T * grid_x
                for o in range(side // 8):
                    put(part, xi, reach + 8 * o, turned[8 * o : 8 * o + 8])
                cells = []
                for f in range(freqs):
                    k, g = (part * freqs + f) // groups, (part * freqs + f) % groups
                    from_l = blocks_of(lambda begin: halo_l[g, pl.ds(xi + begin, 8, stride=nx), :])
                    from_r = blocks_of(lambda begin: halo_r[g, pl.ds(xi + begin, 8, stride=nx), :])
                    cells.append(
                        jnp.where(lane < reach, rolled(from_l, -k * reach, 1), rolled(from_r, reach - k * reach, 1))
                    )
                turned = jnp.concatenate(cells, axis=0).T
                beside_l = turned[:reach] * (grid_x * inside_l)
                beside_r = turned[reach : 2 * reach] * (grid_x * inside_r)
                for o in range(reach // 8):
                    put(part, xi, 8 * o, beside_l[8 * o : 8 * o + 8])
                    put(part, xi, reach + side + 8 * o, beside_r[8 * o : 8 * o + 8])
            return 0

        lax.fori_loop(0, nx, some, 0)

    def slab(n, yi):
        return terms[n, pl.ds(yi * slab_rows, slab_rows), :].reshape(2, nx, 8, 128)

    def x_sum(cells):
        before = pltpu.roll(cells[:, nx - 1 : nx], 1, 3)
        after = pltpu.roll(cells[:, 0:1], 127, 3)
        wide = jnp.concatenate([before, cells, after], axis=1)
        twos = wide[:, :-1] + wide[:, 1:]
        return twos[:, :-1] + twos[:, 1:]

    def next_term(d, n, first):
        ny = blocks_y[d]
        here = slab(n, 0)
        sum_here = x_sum(here)
        sum_first = sum_here
        twos = pltpu.roll(x_sum(slab(n, ny - 1)), 1, 2) + sum_here
        for yi in range(ny):
            if yi + 1 < ny:
                after = slab(n, yi + 1)
                sum_after = x_sum(after)
            else:
                after = None
                sum_after = pltpu.roll(sum_first, 7, 2)
            twos_after = sum_here + sum_after
            nine = twos + twos_after
            rows = pl.ds(yi * slab_rows, slab_rows)
            scale = quarter[d, pl.ds(yi * nx * 8, nx * 8), :].reshape(1, nx, 8, 128)
            if first:
                pair = (0.5 * scale) * nine
            else:
                pair = scale * nine - pair_sum[rows, :].reshape(2, nx, 8, 128)
            pair_sum[rows, :] = pair.reshape(slab_rows, 128)
            terms[n + 1, rows, :] = (pair - here).reshape(slab_rows, 128)
            twos, sum_here, here = twos_after, sum_after, after

    def all_terms(d):
        next_term(d, 0, True)

        def body(n, _):
            next_term(d, n, False)
            return 0

        lax.fori_loop(1, order, body, 0)

    frequency = me_f * freqs + lanes8 // lane_blocks
    omega = (2.0 * math.pi) * (
        LOWEST + (HIGHEST - LOWEST) * (frequency.astype(jnp.float32) + 0.5) / (freqs * fcount)
    )

    def phase_sum(d):
        ny = blocks_y[d]

        def chunk(yi0, count):
            rows = pl.ds(pl.multiple_of(yi0 * slab_rows, 8), count * slab_rows)

            def term(n):
                return terms[n, rows, :].reshape(count, 2, nx, 8, 128)

            slow = jnp.concatenate(
                [
                    slow_rows[d, xi, pl.ds(yi0 + j, 8, stride=ny), :][None]
                    for j in range(count)
                    for xi in range(nx)
                ],
                axis=0,
            )
            angle = (omega * slow).reshape(count, 1, nx, 8, 128)
            square = angle * angle
            cosine = 1.0 + square * (-0.5 + square * (1 / 24.0 + square * (-1 / 720.0)))
            sine = angle * (1.0 + square * (-1 / 6.0 + square * (1 / 120.0 + square * (-1 / 5040.0))))
            double = cosine + cosine
            later = weights[order] * term(order)
            now = weights[order - 1] * term(order - 1) + double * later
            for n in range(order - 2, 0, -1):
                now, later = weights[n] * term(n) + double * now - later, now
            now, later = term(0) + double * now - later, now
            straight = cosine * now - later
            real = straight[:, 0] - sine[:, 0] * now[:, 1]
            imag = straight[:, 1] + sine[:, 0] * now[:, 0]
            for j in range(count):
                for xi in range(nx):
                    rows_buf[0, xi, pl.ds(yi0 + j, 8, stride=ny), :] = real[j, xi]
                    rows_buf[1, xi, pl.ds(yi0 + j, 8, stride=ny), :] = imag[j, xi]

        size = 3

        def body(i, _):
            chunk(i * size, size)
            return 0

        lax.fori_loop(0, ny // size, body, 0)
        if ny % size:
            chunk(ny - ny % size, ny % size)

    def turn(part, xi, h):
        return rows_buf[part, xi, pl.ds(h, side), :].T

    def make_image(d):
        def some(i, _):
            for j in range(3):
                xi = i * 3 + j
                turned = turn(0, xi, around_y[d])
                for o in range(octets):
                    total = turned[8 * o : 8 * o + 8]
                    for f in range(1, freqs):
                        total = total + turned[f * lane_blocks + 8 * o : f * lane_blocks + 8 * o + 8]
                    part_image[d, pl.ds(xi + 8 * nx * o, 8, stride=nx), :] = total
                if d + 1 < depths:
                    ny = blocks_y[d + 1]
                    for yi in range(ny):
                        for part in range(2):
                            rows = pl.ds(pl.multiple_of(((yi * 2 + part) * nx + xi) * 8, 8), 8)
                            terms[0, rows, :] = rows_buf[part, xi, pl.ds(order + yi, 8, stride=ny), :]
            return 0

        lax.fori_loop(0, nx // 3, some, 0)

    def make_natural():
        h = around_y[depths - 1]

        def some(i, _):
            for j in range(3):
                xi = i * 3 + j
                for part in range(2):
                    turned = turn(part, xi, h)
                    for f in range(freqs):
                        for o in range(octets):
                            at = f * lane_blocks + 8 * o
                            natural[part * freqs + f, pl.ds(xi + 8 * nx * o, 8, stride=nx), :] = turned[at : at + 8]
            return 0

        lax.fori_loop(0, nx // 3, some, 0)

    image_stages = [(0, depths - 1), (depths - 1, 1)]
    image_rows = pl.ds(pl.multiple_of(me_f * strip, 8), strip)

    def reduce_copies(stage):
        first, count = image_stages[stage]
        of = pl.ds(first, count)
        return to_peers(
            [
                (
                    part_image.at[of, pl.ds(pl.multiple_of(reach + peer * strip, 8), strip)],
                    image_in.at[k, of],
                )
                for k, peer in enumerate(peers)
            ],
            red_send.at[stage], red_recv.at[stage],
        )

    def cast_image(stage):
        first, count = image_stages[stage]
        of = pl.ds(first, count)
        total = part_image[of, own_rows, :]
        for k in range(fcount - 1):
            total = total + image_in[k, of]
        image_out[of, image_rows, :] = total
        block = image_out.at[of, image_rows]
        return start(to_peers([(block, block)] * (fcount - 1), cast_send.at[stage], cast_recv.at[stage]))

    wait(slow_first)
    build_slow_edges(0)
    halo_first = start(slow_halo_copies(0))
    wait(slow_rest)
    build_slow_edges(1)
    halo_rest = start(slow_halo_copies(1))
    wait(halo_first)
    place_slow_tile(0)
    place_slow_halo(0)
    wait(wave_copies)
    assemble_wave()
    casts = []
    for d in range(depths):
        all_terms(d)
        if d == 0:
            wait(halo_rest)
            for e in range(1, depths):
                place_slow_tile(e)
            place_slow_halo(1)
        phase_sum(d)
        make_image(d)
        if d == depths - 2:
            reduced = start(reduce_copies(0))
    last = start(reduce_copies(1))
    wait(reduced)
    casts += cast_image(0)
    make_natural()
    stores = []
    for f in range(freqs):
        for part in range(2):
            stores.append(
                pltpu.make_async_copy(
                    natural.at[part * freqs + f, pl.ds(reach, side)], out_hbm.at[f, part], store_sem.at[f * 2 + part]
                )
            )
    start(stores)
    wait(last)
    casts += cast_image(1)
    wait(casts)
    image_store = pltpu.make_async_copy(image_out, image_hbm, store_sem.at[batch])
    image_store.start()
    wait(stores)
    image_store.wait()


def per_device(wavefield, velocity):
    freqs, _, side, _ = wavefield.shape
    depths = velocity.shape[0]
    fcount, xcount, ycount = lax.axis_size("freq"), lax.axis_size("gx"), lax.axis_size("gy")
    reach = ORDER * depths
    extent = side + 2 * reach
    nx, ny = extent * freqs // 128, extent // SUB_BLOCKS
    cells = nx * ny * 8
    batch = 2 * freqs
    groups = batch * reach // 128
    strip = side // fcount
    dims = (depths, freqs, side, fcount, xcount, ycount)
    f32 = jnp.float32
    dma = pltpu.SemaphoreType.DMA
    image, extrapolated = pl.pallas_call(
        functools.partial(kernel, dims),
        out_shape=(
            jax.ShapeDtypeStruct((depths, side, side), f32),
            jax.ShapeDtypeStruct(wavefield.shape, f32),
        ),
        in_specs=[pl.BlockSpec(memory_space=pl.ANY)] * 2,
        out_specs=(pl.BlockSpec(memory_space=pl.ANY),) * 2,
        scratch_shapes=[
            pltpu.VMEM((ORDER + 1, 2 * cells, 128), f32),
            pltpu.VMEM((2 * cells, 128), f32),
            pltpu.VMEM((depths, cells, 128), f32),
            pltpu.VMEM((2, nx, extent, 128), f32),
            pltpu.VMEM((depths, nx, extent, 128), f32),
            pltpu.VMEM((batch, extent, 128), f32),
            pltpu.VMEM((groups, side, 128), f32),
            pltpu.VMEM((groups, side, 128), f32),
            pltpu.VMEM((groups, extent, 128), f32),
            pltpu.VMEM((groups, extent, 128), f32),
            pltpu.VMEM((batch, extent, 128), f32),
            pltpu.VMEM((depths, strip, 128), f32),
            pltpu.VMEM((depths, extent, 128), f32),
            pltpu.VMEM((2, side, 128), f32),
            pltpu.VMEM((2, side, 128), f32),
            pltpu.VMEM((2, extent, 128), f32),
            pltpu.VMEM((2, extent, 128), f32),
            pltpu.VMEM((depths, extent, 128), f32),
            pltpu.VMEM((fcount - 1, depths, strip, 128), f32),
            pltpu.VMEM((depths, side, 128), f32),
            dma((batch + 1,)),
            dma((8,)),
            dma((8,)),
            dma((2, fcount - 1)),
            dma((2, fcount - 1)),
            dma((2, 8)),
            dma((2, 8)),
            dma((2, fcount - 1)),
            dma((2, fcount - 1)),
            dma((2, fcount - 1)),
            dma((2, fcount - 1)),
            dma((batch + 1,)),
        ],
        compiler_params=pltpu.CompilerParams(
            collective_id=0, has_side_effects=True, vmem_limit_bytes=56 * 1024 * 1024
        ),
    )(wavefield, velocity)
    weight = shared_weight(ORDER)
    scales = jnp.asarray([weight ** (d + 1) / math.sqrt(freqs * fcount) for d in range(depths)], f32)
    return (image * scales[:, None, None], extrapolated * (weight**depths))


def solution(mesh):
    placed = (P("freq", None, "gx", "gy"), P(None, ("gx", "freq"), "gy"))
    return jax.shard_map(
        per_device,
        mesh=mesh,
        in_specs=placed,
        out_specs=(P(None, "gx", "gy"), P("freq", None, "gx", "gy")),
        check_vma=False,
    )
```

time: 1110 us -> 53.6 us (0.05); the launches traced: 1090 us -> 53.4 us
  starting transfers between devices: 461 us -> 0 us
  other arithmetic: 234 us -> 2.63 us
  local copies, waits for them, and re-layouts: 204 us -> 0.01 us
  blocking collectives: 93.8 us -> 0 us
  waiting for transfers between devices: 81.5 us -> 0 us
  Pallas kernels: 0 us -> 50.1 us
  between operations: 17.7 us -> 0.66 us
    ppermute x128 -> x0, starting transfers between devices: 461 us -> none  [the longest x64 343 us: with_halo(): lax.ppermute(tail, axis, [(i, (i + 1) % count) for i in range(ends)])]
    slice x126 -> x0, local copies, waits for them, and re-layouts: 120 us -> none  [the longest x64 76.7 us: with_halo(): head = lax.slice_in_dim(cells, 0, width, axis=dim)]
    all_gather x4 -> x0, blocking collectives: 93.8 us -> none  [per_device(): slowness_tile = lax.all_gather(velocity[depth], 'freq', axis=0, tiled=True)]
    reduce_sum x4 -> x0, other arithmetic: 78.8 us -> none  [per_device(): partial_image = jnp.sum(real_part, axis=0)]
    add x12 -> x0, other arithmetic: 75.5 us -> none  [the longest x4 37.1 us: add_term(): real_part = real_part + weight * (cosine * part[:, 0] - sine * part[:, 1])]
    ppermute x64 -> x0, local copies, waits for them, and re-layouts: 73.4 us -> none  [the longest x32 38.8 us: with_halo(): lax.ppermute(tail, axis, [(i, (i + 1) % count) for i in range(ends)])]
    concatenate x64 -> x0, other arithmetic: 58.1 us -> none  [with_halo(): jnp.concatenate([lax.ppermute(tail, axis, [(i, (i + 1) % count) for i in...]
    psum x1 -> x0, waiting for transfers between devices: 56.6 us -> none  [per_device(): image_rows.append(lax.psum(partial_image, 'freq') / math.sqrt(freq_total))]
  transfers between devices with their start and end apart: 129 -> 0, of which waited for: 38 -> 0; matrix products, arithmetic and copies ran while one was open for 14% -> 0% of each run, Pallas kernels for 0% -> 0%
where the time goes in v2:
time: 53.6 us; the launch traced here: 53.4 us
  Pallas kernels  50.1 us (93%)
  other arithmetic  2.63 us (5%)
  between operations  0.66 us (1%)
    pallas_call x1, Pallas kernels, per_device(): pl.pallas_call(functools.partial(kernel, dims), out_shape=(jax.ShapeDtype...  50.1 us
    mul x2, other arithmetic, per_device(): return (image * scales[:, None, None], extrapolated * weight ** depths)  2.63 us

profile of v2, /device:TPU:1, one launch (start us, length us, event | category | flops | bytes accessed | tf_op | source)
XLA Modules:
  0.0 53.4 jit_solution(16629278261393143998)
XLA Ops:
  0.6 0.0 copy-start.1
  0.6 50.1 %shard_map.50 = (f32[4,128,128]{2,1,0:T(8,128)}, f32[4,2,128,128]{3,2,1,0:T(8,128)}) custom-call(f32[4,2,128,128]{3,2,1,0:T(8,128)} %wave_hbm.1, f32[4,16,128]{2,1,0:T(8,128)} %vel_hbm.1), custom_call_target="tpu_custom_call" | custom-call | tf_op jit(solution)/shard_map/pallas_call | solution.py:499
  50.8 0.0 copy-start
  50.8 0.0 copy-done.1
  50.8 1.8 %broadcast_multiply_fusion.1 = f32[4,128,128]{2,1,0:T(8,128)} fusion(f32[4,128,128]{2,1,0:T(8,128)} %get-tuple-element.4, f32[4]{0:T(128)S(1)} %copy-done.1), kind=kLoop, calls=%fused_computation.1 | loop fusion | flops 65536 | bytes 524304 | tf_op jit(solution)/shard_map/mul | solution.py:547
  52.6 0.0 copy-done
  52.6 0.8 %broadcast_multiply_fusion = f32[4,2,128,128]{3,2,1,0:T(8,128)} fusion(f32[4,2,128,128]{3,2,1,0:T(8,128)S(1)} %copy-done), kind=kLoop, calls=%fused_computation | loop fusion | flops 131072 | bytes 1048576 | tf_op jit(solution)/shard_map/mul | solution.py:547
Async XLA Ops:
  0.6 50.1 %copy-start.1 = (f32[4]{0:T(128)S(1)}, f32[4]{0:T(128)}, u32[]{:S(2)}) copy-start(f32[4]{0:T(128)} %constant.4.clone) | copy-start | bytes 52
  50.8 1.8 %copy-start = (f32[4,2,128,128]{3,2,1,0:T(8,128)S(1)}, f32[4,2,128,128]{3,2,1,0:T(8,128)}, u32[]{:S(2)}) copy-start(f32[4,2,128,128]{3,2,1,0:T(8,128)} %get-tuple-element.5) | copy-start | bytes 1572868

commit v3 on v2

--- a/solution.py
+++ b/solution.py
@@ -31,12 +31,13 @@
 
 def kernel(
     dims,
-    wave_hbm, vel_hbm, image_hbm, out_hbm,
+    wave_hbm, vel_hbm, image_ref, out_ref,
     terms, pair_sum, quarter, rows_buf, slow_rows, tile, edge_r, edge_l, halo_l, halo_r, natural,
     vel_raw, slow_tile, slow_edge_r, slow_edge_l, slow_halo_l, slow_halo_r,
+    first_edge_r, first_edge_l, first_halo_l, first_halo_r, wide_halo_l, wide_halo_r,
     part_image, image_in, image_out,
-    load_sem, wave_send, wave_recv, vel_send, vel_recv, velh_send, velh_recv,
-    red_send, red_recv, cast_send, cast_recv, store_sem,
+    load_sem, wave_send, wave_recv, vel_send, vel_recv, velh_send, velh_recv, rows_send, rows_recv,
+    red_send, red_recv, cast_send, cast_recv,
 ):
     depths, freqs, side, fcount, xcount, ycount = dims
     order = ORDER
@@ -120,7 +121,7 @@
                 src_ref=source, dst_ref=target, send_sem=send_sem.at[k], recv_sem=recv_sem.at[k],
                 device_id=around[k], device_id_type=MESH,
             )
-            for k, (source, target) in enumerate(pairs)
+            for k, (source, target) in [(k, pair) for k, pair in enumerate(pairs) if pair is not None]
         ]
 
     def to_peers(pairs, send_sem, recv_sem):
@@ -155,6 +156,7 @@
         wave_send, wave_recv,
     )
     stages = [(0, 1), (1, depths - 1)]
+    ahead = [reach - order * (d + 1) for d in range(depths)]
 
     def slow_peer_copies(stage):
         first, count = stages[stage]
@@ -162,35 +164,64 @@
         return to_peers([(block, block)] * (fcount - 1), vel_send.at[stage], vel_recv.at[stage])
 
     def slow_halo_copies(stage):
-        first, count = stages[stage]
-        of = pl.ds(first, count)
-        return to_neighbours(
-            [
-                (slow_tile.at[of, own_head], slow_tile.at[of, high]),
-                (slow_tile.at[of, own_tail], slow_tile.at[of, low]),
-                (slow_edge_r.at[stage], slow_halo_l.at[stage, mid]),
-                (slow_edge_l.at[stage], slow_halo_r.at[stage, mid]),
-                (slow_edge_r.at[stage, head], slow_halo_l.at[stage, high]),
-                (slow_edge_r.at[stage, tail], slow_halo_l.at[stage, low]),
-                (slow_edge_l.at[stage, head], slow_halo_r.at[stage, high]),
-                (slow_edge_l.at[stage, tail], slow_halo_r.at[stage, low]),
-            ],
-            velh_send.at[stage], velh_recv.at[stage],
-        )
+        copies = []
+        for k, d in enumerate([0] if stage == 0 else range(1, depths - 1)):
+            w = ahead[d]
+            rows = [
+                (slow_tile.at[d, pl.ds(reach, w)], slow_tile.at[d, pl.ds(reach + side, w)]),
+                (slow_tile.at[d, pl.ds(reach + side - w, w)], slow_tile.at[d, pl.ds(reach - w, w)]),
+            ]
+            copies += to_neighbours(rows, rows_send.at[stage + k], rows_recv.at[stage + k])
+        if stage == 0:
+            sides = [(first_edge_r, first_halo_l.at[1]), (first_edge_l, first_halo_r.at[1])]
+            for edge, halo in ((first_edge_r, first_halo_l), (first_edge_l, first_halo_r)):
+                sides += [(edge, halo.at[2]), (edge, halo.at[0])]
+        else:
+            w = ahead[1]
+            sides = [(slow_edge_r, slow_halo_l.at[mid]), (slow_edge_l, slow_halo_r.at[mid])]
+            for edge, halo in ((slow_edge_r, slow_halo_l), (slow_edge_l, slow_halo_r)):
+                sides += [
+                    (edge.at[pl.ds(0, w)], halo.at[pl.ds(reach + side, w)]),
+                    (edge.at[pl.ds(side - w, w)], halo.at[pl.ds(reach - w, w)]),
+                ]
+        return copies + to_neighbours([None, None] + sides, velh_send.at[stage], velh_recv.at[stage])
 
     def build_slow_edges(stage):
+        if stage == 0:
+            for target, source in ((first_edge_r, side - reach), (first_edge_l, 0)):
+                made = None
+                for j in range(side // reach):
+                    moved = rolled(slow_tile[0, pl.ds(reach + reach * j, reach), :], reach * j - source, 1)
+                    made = moved if made is None else jnp.where(lane >= reach * j, moved, made)
+                target[...] = made
+            return
         first, count = stages[stage]
         for target, source in ((slow_edge_r, side - reach), (slow_edge_l, 0)):
             made = None
             for j in range(count):
                 moved = rolled(slow_tile[first + j, pl.ds(reach, side), :], reach * j - source, 1)
                 made = moved if made is None else jnp.where(lane >= reach * j, moved, made)
-            target[stage] = made
+            target[...] = made
+
+    def unpack_first_halo():
+        for halo, target in ((first_halo_l, wide_halo_l), (first_halo_r, wide_halo_r)):
+            target[pl.ds(0, reach), :] = rolled(halo[0], -(side - reach), 1)
+            for j in range(side // reach):
+                target[pl.ds(reach + reach * j, reach), :] = rolled(halo[1], -reach * j, 1)
+            target[pl.ds(reach + side, reach), :] = halo[2]
+
+    for d in range(depths):
+        rest = reach - (ahead[d] if d < depths - 1 else 0)
+        slow_tile[d, pl.ds(0, rest), :] = jnp.zeros((rest, side), jnp.float32)
+        slow_tile[d, pl.ds(extent - rest, rest), :] = jnp.zeros((rest, side), jnp.float32)
+    rest = reach - ahead[1]
+    for halo in (slow_halo_l, slow_halo_r):
+        halo[pl.ds(0, rest), :] = jnp.zeros((rest, side), jnp.float32)
+        halo[pl.ds(extent - rest, rest), :] = jnp.zeros((rest, side), jnp.float32)
 
     pl.semaphore_wait(barrier, len(around) + len(peers))
     slow_first = start(slow_peer_copies(0))
     start(wave_copies)
-    slow_rest = start(slow_peer_copies(1))
 
     lanes8 = lax.broadcasted_iota(jnp.int32, (8, 128), 1)
     subs8 = lax.broadcasted_iota(jnp.int32, (8, 128), 0)
@@ -199,7 +230,7 @@
         x = me_x * side - reach + lax.rem(lanes, lane_blocks) * nx + xi
         return (x >= 0) & (x < xcount * side)
 
-    for d in range(depths):
+    def fill_quarters(d):
         def fill_quarter(yi, _):
             y = me_y * side - around_y[d] + subs8 * blocks_y[d] + yi
             inside_y = jnp.where((y >= 0) & (y < ycount * side), 0.25, 0.0)
@@ -210,6 +241,10 @@
 
         lax.fori_loop(0, blocks_y[d], fill_quarter, 0)
 
+    def fill_all_quarters():
+        for d in range(depths):
+            fill_quarters(d)
+
     def blocks_of(load):
         return jnp.concatenate([load(8 * nx * o) for o in range(octets)], axis=0)
 
@@ -220,10 +255,14 @@
 
     def place_slow_halo(stage):
         first, count = stages[stage]
+        if stage == 0:
+            edges_l, edges_r = wide_halo_l, wide_halo_r
+        else:
+            edges_l, edges_r = slow_halo_l, slow_halo_r
         for pair in range(0, count, 2):
             for xi in range(nx):
-                from_l = blocks_of(lambda begin: slow_halo_l[stage, pl.ds(xi + begin, 8, stride=nx), :])
-                from_r = blocks_of(lambda begin: slow_halo_r[stage, pl.ds(xi + begin, 8, stride=nx), :])
+                from_l = blocks_of(lambda begin: edges_l[pl.ds(xi + begin, 8, stride=nx), :])
+                from_r = blocks_of(lambda begin: edges_r[pl.ds(xi + begin, 8, stride=nx), :])
                 made = jnp.where(lane < reach, rolled(from_l, -reach * pair, 1), rolled(from_r, reach - reach * pair, 1))
                 if pair + 1 < count:
                     made = jnp.where(lane < 2 * reach, made, rolled(from_l, reach * (1 - pair), 1))
@@ -409,6 +448,9 @@
             return 0
 
         lax.fori_loop(0, nx // 3, some, 0)
+        for f in range(freqs):
+            for part in range(2):
+                out_ref[f, part] = natural[part * freqs + f, pl.ds(reach, side), :] * shared_weight(order) ** depths
 
     image_stages = [(0, depths - 1), (depths - 1, 1)]
     image_rows = pl.ds(pl.multiple_of(me_f * strip, 8), strip)
@@ -433,25 +475,30 @@
         total = part_image[of, own_rows, :]
         for k in range(fcount - 1):
             total = total + image_in[k, of]
-        image_out[of, image_rows, :] = total
+        for d in range(first, first + count):
+            scale = shared_weight(order) ** (d + 1) / math.sqrt(freqs * fcount)
+            image_out[d, image_rows, :] = total[d - first] * scale
         block = image_out.at[of, image_rows]
         return start(to_peers([(block, block)] * (fcount - 1), cast_send.at[stage], cast_recv.at[stage]))
 
     wait(slow_first)
     build_slow_edges(0)
     halo_first = start(slow_halo_copies(0))
-    wait(slow_rest)
-    build_slow_edges(1)
-    halo_rest = start(slow_halo_copies(1))
+    slow_rest = start(slow_peer_copies(1))
+    fill_all_quarters()
     wait(halo_first)
+    unpack_first_halo()
     place_slow_tile(0)
     place_slow_halo(0)
     wait(wave_copies)
     assemble_wave()
+    wait(slow_rest)
+    build_slow_edges(1)
+    halo_rest = start(slow_halo_copies(1))
     casts = []
     for d in range(depths):
         all_terms(d)
-        if d == 0:
+        if d == 1:
             wait(halo_rest)
             for e in range(1, depths):
                 place_slow_tile(e)
@@ -464,22 +511,10 @@
     wait(reduced)
     casts += cast_image(0)
     make_natural()
-    stores = []
-    for f in range(freqs):
-        for part in range(2):
-            stores.append(
-                pltpu.make_async_copy(
-                    natural.at[part * freqs + f, pl.ds(reach, side)], out_hbm.at[f, part], store_sem.at[f * 2 + part]
-                )
-            )
-    start(stores)
     wait(last)
     casts += cast_image(1)
     wait(casts)
-    image_store = pltpu.make_async_copy(image_out, image_hbm, store_sem.at[batch])
-    image_store.start()
-    wait(stores)
-    image_store.wait()
+    image_ref[...] = image_out[...]
 
 
 def per_device(wavefield, velocity):
@@ -499,11 +534,11 @@
     image, extrapolated = pl.pallas_call(
         functools.partial(kernel, dims),
         out_shape=(
-            jax.ShapeDtypeStruct((depths, side, side), f32),
-            jax.ShapeDtypeStruct(wavefield.shape, f32),
+            pltpu.VMEM((depths, side, side), f32),
+            pltpu.VMEM(wavefield.shape, f32),
         ),
-        in_specs=[pl.BlockSpec(memory_space=pl.ANY)] * 2,
-        out_specs=(pl.BlockSpec(memory_space=pl.ANY),) * 2,
+        in_specs=[pl.BlockSpec(memory_space=pltpu.HBM)] * 2,
+        out_specs=(pl.BlockSpec(memory_space=pltpu.VMEM),) * 2,
         scratch_shapes=[
             pltpu.VMEM((ORDER + 1, 2 * cells, 128), f32),
             pltpu.VMEM((2 * cells, 128), f32),
@@ -518,10 +553,16 @@
             pltpu.VMEM((batch, extent, 128), f32),
             pltpu.VMEM((depths, strip, 128), f32),
             pltpu.VMEM((depths, extent, 128), f32),
-            pltpu.VMEM((2, side, 128), f32),
-            pltpu.VMEM((2, side, 128), f32),
-            pltpu.VMEM((2, extent, 128), f32),
-            pltpu.VMEM((2, extent, 128), f32),
+            pltpu.VMEM((side, 128), f32),
+            pltpu.VMEM((side, 128), f32),
+            pltpu.VMEM((extent, 128), f32),
+            pltpu.VMEM((extent, 128), f32),
+            pltpu.VMEM((reach, 128), f32),
+            pltpu.VMEM((reach, 128), f32),
+            pltpu.VMEM((3, reach, 128), f32),
+            pltpu.VMEM((3, reach, 128), f32),
+            pltpu.VMEM((extent, 128), f32),
+            pltpu.VMEM((extent, 128), f32),
             pltpu.VMEM((depths, extent, 128), f32),
             pltpu.VMEM((fcount - 1, depths, strip, 128), f32),
             pltpu.VMEM((depths, side, 128), f32),
@@ -532,19 +573,18 @@
             dma((2, fcount - 1)),
             dma((2, 8)),
             dma((2, 8)),
+            dma((depths - 1, 2)),
+            dma((depths - 1, 2)),
             dma((2, fcount - 1)),
             dma((2, fcount - 1)),
             dma((2, fcount - 1)),
             dma((2, fcount - 1)),
-            dma((batch + 1,)),
         ],
         compiler_params=pltpu.CompilerParams(
-            collective_id=0, has_side_effects=True, vmem_limit_bytes=56 * 1024 * 1024
+            collective_id=0, has_side_effects=True, vmem_limit_bytes=66_000_000
         ),
     )(wavefield, velocity)
-    weight = shared_weight(ORDER)
-    scales = jnp.asarray([weight ** (d + 1) / math.sqrt(freqs * fcount) for d in range(depths)], f32)
-    return (image * scales[:, None, None], extrapolated * (weight**depths))
+    return (image, extrapolated)
 
 
 def solution(mesh):

time: 53.6 us -> 48.7 us (0.909)
  Pallas kernels: 50.1 us -> 46.4 us
  other arithmetic: 2.63 us -> 0 us
  local copies, waits for them, and re-layouts: 0.01 us -> 1.5 us
    pallas_call x1, Pallas kernels: 50.1 us -> 46.4 us  [per_device(): pl.pallas_call(functools.partial(kernel, dims), out_shape=(pltpu.VMEM((de...]
    mul x2 -> x0, other arithmetic: 2.63 us -> none  [per_device(): return (image * scales[:, None, None], extrapolated * weight ** depths)]
    unnamed x4 -> x2, local copies, waits for them, and re-layouts: 0.01 us -> 1.5 us
where the time goes in v3:
time: 48.7 us; the launch traced here: 48.5 us
  Pallas kernels  46.4 us (95%)
  local copies, waits for them, and re-layouts  1.5 us (3%)
  between operations  0.64 us (1%)
    pallas_call x1, Pallas kernels, per_device(): pl.pallas_call(functools.partial(kernel, dims), out_shape=(pltpu.VMEM((de...  46.4 us
    unnamed x2, local copies, waits for them, and re-layouts  1.5 us

profile of v3, /device:TPU:1, one launch (start us, length us, event | category | flops | bytes accessed | tf_op | source)
XLA Modules:
  0.0 48.5 jit_solution(8784396589624992079)
XLA Ops:
  0.6 46.4 %shard_map.41 = (f32[4,128,128]{2,1,0:T(8,128)S(1)}, f32[4,2,128,128]{3,2,1,0:T(8,128)S(1)}) custom-call(f32[4,2,128,128]{3,2,1,0:T(8,128)} %wave_hbm.1, f32[4,16,128]{2,1,0:T(8,128)} %vel_hbm.1), custom_call_target="tpu_custom_call" | custom-call | tf_op jit(solution)/shard_map/pallas_call | solution.py:534
  47.0 0.7 %copy.6 = f32[4,128,128]{2,1,0:T(8,128)} copy(f32[4,128,128]{2,1,0:T(8,128)S(1)} %get-tuple-element.2) | data formatting | bytes 524288
  47.7 0.8 %copy.7 = f32[4,2,128,128]{3,2,1,0:T(8,128)} copy(f32[4,2,128,128]{3,2,1,0:T(8,128)S(1)} %get-tuple-element.3) | data formatting | bytes 1048576

commit v4 on v3

--- a/solution.py
+++ b/solution.py
@@ -285,36 +285,55 @@
             begin = ((yi * 2 + part) * nx + xi) * 8 + yb
             terms[0, pl.ds(begin, 8, stride=slab_rows), :] = block
 
-        def some(xi, _):
-            grid_x = jnp.where(inside_x(xi, lane), 1.0, 0.0)
-            for part in range(2):
-                cells = jnp.concatenate(
-                    [
-                        blocks_of(lambda begin: tile[part * freqs + f, pl.ds(xi + begin, 8, stride=nx), :])
-                        for f in range(freqs)
-                    ],
-                    axis=0,
-                )
-                turned = cells.T * grid_x
-                for o in range(side // 8):
-                    put(part, xi, reach + 8 * o, turned[8 * o : 8 * o + 8])
+        def middle(i, _):
+            for j in range(3):
+                xi = i * 3 + j
+                grid_x = jnp.where(inside_x(xi, lane), 1.0, 0.0)
+                for part in range(2):
+                    cells = jnp.concatenate(
+                        [
+                            blocks_of(lambda begin: tile[part * freqs + f, pl.ds(xi + begin, 8, stride=nx), :])
+                            for f in range(freqs)
+                        ],
+                        axis=0,
+                    )
+                    turned = cells.T * grid_x
+                    for o in range(side // 8):
+                        put(part, xi, reach + 8 * o, turned[8 * o : 8 * o + 8])
+            return 0
+
+        def beside(i, _):
+            for j in range(3):
+                xi = i * 3 + j
+                grid_x = jnp.where(inside_x(xi, lane), 1.0, 0.0)
                 cells = []
                 for f in range(freqs):
-                    k, g = (part * freqs + f) // groups, (part * freqs + f) % groups
-                    from_l = blocks_of(lambda begin: halo_l[g, pl.ds(xi + begin, 8, stride=nx), :])
-                    from_r = blocks_of(lambda begin: halo_r[g, pl.ds(xi + begin, 8, stride=nx), :])
-                    cells.append(
-                        jnp.where(lane < reach, rolled(from_l, -k * reach, 1), rolled(from_r, reach - k * reach, 1))
-                    )
+                    both = []
+                    for part in range(2):
+                        k, g = (part * freqs + f) // groups, (part * freqs + f) % groups
+                        from_l = blocks_of(lambda begin: halo_l[g, pl.ds(xi + begin, 8, stride=nx), :])
+                        from_r = blocks_of(lambda begin: halo_r[g, pl.ds(xi + begin, 8, stride=nx), :])
+                        at = 2 * reach * part
+                        both.append(
+                            jnp.where(
+                                lane < at + reach, rolled(from_l, at - k * reach, 1), rolled(from_r, at + reach - k * reach, 1)
+                            )
+                        )
+                    cells.append(jnp.where(lane < 2 * reach, both[0], both[1]))
                 turned = jnp.concatenate(cells, axis=0).T
-                beside_l = turned[:reach] * (grid_x * inside_l)
-                beside_r = turned[reach : 2 * reach] * (grid_x * inside_r)
-                for o in range(reach // 8):
-                    put(part, xi, 8 * o, beside_l[8 * o : 8 * o + 8])
-                    put(part, xi, reach + side + 8 * o, beside_r[8 * o : 8 * o + 8])
+                for part in range(2):
+                    at = 2 * reach * part
+                    beside_l = turned[at : at + reach] * (grid_x * inside_l)
+                    beside_r = turned[at + reach : at + 2 * reach] * (grid_x * inside_r)
+                    for o in range(reach // 8):
+                        put(part, xi, 8 * o, beside_l[8 * o : 8 * o + 8])
+                        put(part, xi, reach + side + 8 * o, beside_r[8 * o : 8 * o + 8])
             return 0
 
-        lax.fori_loop(0, nx, some, 0)
+        wait(wave_copies[:2])
+        lax.fori_loop(0, nx // 3, middle, 0)
+        wait(wave_copies[2:])
+        lax.fori_loop(0, nx // 3, beside, 0)
 
     def slab(n, yi):
         return terms[n, pl.ds(yi * slab_rows, slab_rows), :].reshape(2, nx, 8, 128)
@@ -486,18 +505,18 @@
     halo_first = start(slow_halo_copies(0))
     slow_rest = start(slow_peer_copies(1))
     fill_all_quarters()
-    wait(halo_first)
-    unpack_first_halo()
-    place_slow_tile(0)
-    place_slow_halo(0)
-    wait(wave_copies)
     assemble_wave()
-    wait(slow_rest)
-    build_slow_edges(1)
-    halo_rest = start(slow_halo_copies(1))
     casts = []
     for d in range(depths):
         all_terms(d)
+        if d == 0:
+            wait(halo_first)
+            unpack_first_halo()
+            place_slow_tile(0)
+            place_slow_halo(0)
+            wait(slow_rest)
+            build_slow_edges(1)
+            halo_rest = start(slow_halo_copies(1))
         if d == 1:
             wait(halo_rest)
             for e in range(1, depths):

time: 48.7 us -> 46.8 us (0.961)
  Pallas kernels: 46.4 us -> 44.1 us
    pallas_call x1, Pallas kernels: 46.4 us -> 44.1 us  [per_device(): pl.pallas_call(functools.partial(kernel, dims), out_shape=(pltpu.VMEM((de...]
where the time goes in v4:
time: 46.8 us; the launch traced here: 46.2 us
  Pallas kernels  44.1 us (94%)
  local copies, waits for them, and re-layouts  1.5 us (3%)
  between operations  0.64 us (1%)
    pallas_call x1, Pallas kernels, per_device(): pl.pallas_call(functools.partial(kernel, dims), out_shape=(pltpu.VMEM((de...  44.1 us
    unnamed x2, local copies, waits for them, and re-layouts  1.5 us

profile of v4, /device:TPU:1, one launch (start us, length us, event | category | flops | bytes accessed | tf_op | source)
XLA Modules:
  0.0 46.2 jit_solution(11391534688905983953)
XLA Ops:
  0.6 44.1 %shard_map.41 = (f32[4,128,128]{2,1,0:T(8,128)S(1)}, f32[4,2,128,128]{3,2,1,0:T(8,128)S(1)}) custom-call(f32[4,2,128,128]{3,2,1,0:T(8,128)} %wave_hbm.1, f32[4,16,128]{2,1,0:T(8,128)} %vel_hbm.1), custom_call_target="tpu_custom_call" | custom-call | tf_op jit(solution)/shard_map/pallas_call | solution.py:553
  44.7 0.7 %copy.6 = f32[4,128,128]{2,1,0:T(8,128)} copy(f32[4,128,128]{2,1,0:T(8,128)S(1)} %get-tuple-element.2) | data formatting | bytes 524288
  45.4 0.8 %copy.7 = f32[4,2,128,128]{3,2,1,0:T(8,128)} copy(f32[4,2,128,128]{3,2,1,0:T(8,128)S(1)} %get-tuple-element.3) | data formatting | bytes 1048576

commit v5 on v4

--- a/solution.py
+++ b/solution.py
@@ -117,10 +117,10 @@
 
     def to_neighbours(pairs, send_sem, recv_sem):
         return [
-            pltpu.make_async_remote_copy(
+            (k, pltpu.make_async_remote_copy(
                 src_ref=source, dst_ref=target, send_sem=send_sem.at[k], recv_sem=recv_sem.at[k],
                 device_id=around[k], device_id_type=MESH,
-            )
+            ))
             for k, (source, target) in [(k, pair) for k, pair in enumerate(pairs) if pair is not None]
         ]
 
@@ -141,6 +141,63 @@
     def wait(copies):
         for copy in copies:
             copy.wait()
+
+    has_left, has_right = me_y > 0, me_y < ycount - 1
+    rightwards, leftwards = (2, 4, 5), (3, 6, 7)
+
+    def start_near(copies):
+        for k, copy in copies:
+            if k < 2:
+                copy.start()
+
+        @pl.when(has_right)
+        def _():
+            for k, copy in copies:
+                if k in rightwards:
+                    copy.start()
+
+        @pl.when(has_left)
+        def _():
+            for k, copy in copies:
+                if k in leftwards:
+                    copy.start()
+
+        return copies
+
+    def wait_near(copies):
+        for k, copy in copies:
+            if k < 2:
+                copy.wait()
+        if all(k < 2 for k, _ in copies):
+            return
+
+        @pl.when(has_right)
+        def _():
+            for k, copy in copies:
+                if k in rightwards:
+                    copy.wait_send()
+                if k in leftwards:
+                    copy.wait_recv()
+
+        @pl.when(has_left)
+        def _():
+            for k, copy in copies:
+                if k in leftwards:
+                    copy.wait_send()
+                if k in rightwards:
+                    copy.wait_recv()
+
+    def clear(refs):
+        for ref in refs:
+            ref[...] = jnp.zeros(ref.shape, jnp.float32)
+
+    @pl.when(me_y == 0)
+    def _():
+        clear((halo_l, first_halo_l, slow_halo_l))
+
+    @pl.when(me_y == ycount - 1)
+    def _():
+        clear((halo_r, first_halo_r, slow_halo_r))
 
     wave_copies = to_neighbours(
         [
@@ -221,7 +278,7 @@
 
     pl.semaphore_wait(barrier, len(around) + len(peers))
     slow_first = start(slow_peer_copies(0))
-    start(wave_copies)
+    start_near(wave_copies)
 
     lanes8 = lax.broadcasted_iota(jnp.int32, (8, 128), 1)
     subs8 = lax.broadcasted_iota(jnp.int32, (8, 128), 0)
@@ -330,9 +387,9 @@
                         put(part, xi, reach + side + 8 * o, beside_r[8 * o : 8 * o + 8])
             return 0
 
-        wait(wave_copies[:2])
+        wait_near(wave_copies[:2])
         lax.fori_loop(0, nx // 3, middle, 0)
-        wait(wave_copies[2:])
+        wait_near(wave_copies[2:])
         lax.fori_loop(0, nx // 3, beside, 0)
 
     def slab(n, yi):
@@ -502,7 +559,7 @@
 
     wait(slow_first)
     build_slow_edges(0)
-    halo_first = start(slow_halo_copies(0))
+    halo_first = start_near(slow_halo_copies(0))
     slow_rest = start(slow_peer_copies(1))
     fill_all_quarters()
     assemble_wave()
@@ -510,15 +567,15 @@
     for d in range(depths):
         all_terms(d)
         if d == 0:
-            wait(halo_first)
+            wait_near(halo_first)
             unpack_first_halo()
             place_slow_tile(0)
             place_slow_halo(0)
             wait(slow_rest)
             build_slow_edges(1)
-            halo_rest = start(slow_halo_copies(1))
+            halo_rest = start_near(slow_halo_copies(1))
         if d == 1:
-            wait(halo_rest)
+            wait_near(halo_rest)
             for e in range(1, depths):
                 place_slow_tile(e)
             place_slow_halo(1)

time: 46.8 us -> 44.7 us (0.955)
  Pallas kernels: 44.1 us -> 42.4 us
    pallas_call x1, Pallas kernels: 44.1 us -> 42.4 us  [per_device(): pl.pallas_call(functools.partial(kernel, dims), out_shape=(pltpu.VMEM((de...]
where the time goes in v5:
time: 44.7 us; the launch traced here: 44.5 us
  Pallas kernels  42.4 us (95%)
  local copies, waits for them, and re-layouts  1.5 us (3%)
  between operations  0.64 us (1%)
    pallas_call x1, Pallas kernels, per_device(): pl.pallas_call(functools.partial(kernel, dims), out_shape=(pltpu.VMEM((de...  42.4 us
    unnamed x2, local copies, waits for them, and re-layouts  1.5 us

profile of v5, /device:TPU:1, one launch (start us, length us, event | category | flops | bytes accessed | tf_op | source)
XLA Modules:
  0.0 44.5 jit_solution(10071311552256977630)
XLA Ops:
  0.6 42.4 %shard_map.41 = (f32[4,128,128]{2,1,0:T(8,128)S(1)}, f32[4,2,128,128]{3,2,1,0:T(8,128)S(1)}) custom-call(f32[4,2,128,128]{3,2,1,0:T(8,128)} %wave_hbm.1, f32[4,16,128]{2,1,0:T(8,128)} %vel_hbm.1), custom_call_target="tpu_custom_call" | custom-call | tf_op jit(solution)/shard_map/pallas_call | solution.py:610
  43.0 0.7 %copy.6 = f32[4,128,128]{2,1,0:T(8,128)} copy(f32[4,128,128]{2,1,0:T(8,128)S(1)} %get-tuple-element.2) | data formatting | bytes 524288
  43.7 0.8 %copy.7 = f32[4,2,128,128]{3,2,1,0:T(8,128)} copy(f32[4,2,128,128]{3,2,1,0:T(8,128)S(1)} %get-tuple-element.3) | data formatting | bytes 1048576

commit v6 on v4

--- a/solution.py
+++ b/solution.py
@@ -70,9 +70,23 @@
     ]
     peers = [mod(me_f + k, fcount) for k in range(1, fcount)]
 
+    has_up, has_down = me_x > 0, me_x < xcount - 1
+    has_left, has_right = me_y > 0, me_y < ycount - 1
+    present = [
+        has_up, has_down, has_right, has_left,
+        has_up & has_right, has_down & has_right, has_up & has_left, has_down & has_left,
+    ]
+    opposite = [1, 0, 3, 2, 7, 6, 5, 4]
+
     barrier = pltpu.get_barrier_semaphore()
-    for device in around:
-        pl.semaphore_signal(barrier, inc=1, device_id=device, device_id_type=MESH)
+    greeted = jnp.int32(fcount - 1)
+    for way, device in enumerate(around):
+        greeted = greeted + jnp.where(present[way], 1, 0)
+
+        @pl.when(present[way])
+        def _():
+            pl.semaphore_signal(barrier, inc=1, device_id=device, device_id_type=MESH)
+
     for peer in peers:
         pl.semaphore_signal(barrier, inc=1, device_id={"freq": peer}, device_id_type=MESH)
 
@@ -117,10 +131,10 @@
 
     def to_neighbours(pairs, send_sem, recv_sem):
         return [
-            pltpu.make_async_remote_copy(
+            (k, pltpu.make_async_remote_copy(
                 src_ref=source, dst_ref=target, send_sem=send_sem.at[k], recv_sem=recv_sem.at[k],
                 device_id=around[k], device_id_type=MESH,
-            )
+            ))
             for k, (source, target) in [(k, pair) for k, pair in enumerate(pairs) if pair is not None]
         ]
 
@@ -141,6 +155,55 @@
     def wait(copies):
         for copy in copies:
             copy.wait()
+
+    def start_near(copies):
+        for way in range(8):
+            here = [copy for k, copy in copies if k == way]
+            if here:
+
+                @pl.when(present[way])
+                def _():
+                    for copy in here:
+                        copy.start()
+
+        return copies
+
+    def wait_near(copies):
+        for way in range(8):
+            sent = [copy for k, copy in copies if k == way]
+            received = [copy for k, copy in copies if k == opposite[way]]
+            if sent or received:
+
+                @pl.when(present[way])
+                def _():
+                    for copy in sent:
+                        copy.wait_send()
+                    for copy in received:
+                        copy.wait_recv()
+
+    def clear(refs):
+        for ref in refs:
+            ref[...] = jnp.zeros(ref.shape, jnp.float32)
+
+    @pl.when(me_y == 0)
+    def _():
+        clear((halo_l, first_halo_l, slow_halo_l))
+
+    @pl.when(me_y == ycount - 1)
+    def _():
+        clear((halo_r, first_halo_r, slow_halo_r))
+
+    @pl.when(me_x == 0)
+    def _():
+        clear((tile.at[:, low], slow_tile.at[:, low]))
+        for wide, first, later in ((halo_l, first_halo_l, slow_halo_l), (halo_r, first_halo_r, slow_halo_r)):
+            clear((wide.at[:, low], first.at[0], later.at[low]))
+
+    @pl.when(me_x == xcount - 1)
+    def _():
+        clear((tile.at[:, high], slow_tile.at[:, high]))
+        for wide, first, later in ((halo_l, first_halo_l, slow_halo_l), (halo_r, first_halo_r, slow_halo_r)):
+            clear((wide.at[:, high], first.at[2], later.at[high]))
 
     wave_copies = to_neighbours(
         [
@@ -219,9 +282,9 @@
         halo[pl.ds(0, rest), :] = jnp.zeros((rest, side), jnp.float32)
         halo[pl.ds(extent - rest, rest), :] = jnp.zeros((rest, side), jnp.float32)
 
-    pl.semaphore_wait(barrier, len(around) + len(peers))
+    pl.semaphore_wait(barrier, greeted)
     slow_first = start(slow_peer_copies(0))
-    start(wave_copies)
+    start_near(wave_copies)
 
     lanes8 = lax.broadcasted_iota(jnp.int32, (8, 128), 1)
     subs8 = lax.broadcasted_iota(jnp.int32, (8, 128), 0)
@@ -330,9 +393,9 @@
                         put(part, xi, reach + side + 8 * o, beside_r[8 * o : 8 * o + 8])
             return 0
 
-        wait(wave_copies[:2])
+        wait_near(wave_copies[:2])
         lax.fori_loop(0, nx // 3, middle, 0)
-        wait(wave_copies[2:])
+        wait_near(wave_copies[2:])
         lax.fori_loop(0, nx // 3, beside, 0)
 
     def slab(n, yi):
@@ -502,7 +565,7 @@
 
     wait(slow_first)
     build_slow_edges(0)
-    halo_first = start(slow_halo_copies(0))
+    halo_first = start_near(slow_halo_copies(0))
     slow_rest = start(slow_peer_copies(1))
     fill_all_quarters()
     assemble_wave()
@@ -510,15 +573,15 @@
     for d in range(depths):
         all_terms(d)
         if d == 0:
-            wait(halo_first)
+            wait_near(halo_first)
             unpack_first_halo()
             place_slow_tile(0)
             place_slow_halo(0)
             wait(slow_rest)
             build_slow_edges(1)
-            halo_rest = start(slow_halo_copies(1))
+            halo_rest = start_near(slow_halo_copies(1))
         if d == 1:
-            wait(halo_rest)
+            wait_near(halo_rest)
             for e in range(1, depths):
                 place_slow_tile(e)
             place_slow_halo(1)

time: 46.8 us -> 42.6 us (0.910)
  Pallas kernels: 44.1 us -> 40.3 us
    pallas_call x1, Pallas kernels: 44.1 us -> 40.3 us  [per_device(): pl.pallas_call(functools.partial(kernel, dims), out_shape=(pltpu.VMEM((de...]
where the time goes in v6:
time: 42.6 us; the launch traced here: 42.5 us
  Pallas kernels  40.3 us (95%)
  local copies, waits for them, and re-layouts  1.5 us (4%)
  between operations  0.64 us (2%)
    pallas_call x1, Pallas kernels, per_device(): pl.pallas_call(functools.partial(kernel, dims), out_shape=(pltpu.VMEM((de...  40.3 us
    unnamed x2, local copies, waits for them, and re-layouts  1.5 us

profile of v6, /device:TPU:1, one launch (start us, length us, event | category | flops | bytes accessed | tf_op | source)
XLA Modules:
  0.0 42.5 jit_solution(15209995680359053586)
XLA Ops:
  0.6 40.3 %shard_map.41 = (f32[4,128,128]{2,1,0:T(8,128)S(1)}, f32[4,2,128,128]{3,2,1,0:T(8,128)S(1)}) custom-call(f32[4,2,128,128]{3,2,1,0:T(8,128)} %wave_hbm.1, f32[4,16,128]{2,1,0:T(8,128)} %vel_hbm.1), custom_call_target="tpu_custom_call" | custom-call | tf_op jit(solution)/shard_map/pallas_call | solution.py:616
  41.0 0.7 %copy.6 = f32[4,128,128]{2,1,0:T(8,128)} copy(f32[4,128,128]{2,1,0:T(8,128)S(1)} %get-tuple-element.2) | data formatting | bytes 524288
  41.7 0.8 %copy.7 = f32[4,2,128,128]{3,2,1,0:T(8,128)} copy(f32[4,2,128,128]{3,2,1,0:T(8,128)S(1)} %get-tuple-element.3) | data formatting | bytes 1048576

commit v7 on v6

--- a/solution.py
+++ b/solution.py
@@ -467,7 +467,7 @@
             angle = (omega * slow).reshape(count, 1, nx, 8, 128)
             square = angle * angle
             cosine = 1.0 + square * (-0.5 + square * (1 / 24.0 + square * (-1 / 720.0)))
-            sine = angle * (1.0 + square * (-1 / 6.0 + square * (1 / 120.0 + square * (-1 / 5040.0))))
+            sine = angle * (1.0 + square * (-0.16666656 + square * 0.00831999))
             double = cosine + cosine
             later = weights[order] * term(order)
             now = weights[order - 1] * term(order - 1) + double * later
@@ -482,7 +482,7 @@
                     rows_buf[0, xi, pl.ds(yi0 + j, 8, stride=ny), :] = real[j, xi]
                     rows_buf[1, xi, pl.ds(yi0 + j, 8, stride=ny), :] = imag[j, xi]
 
-        size = 3
+        size = 4
 
         def body(i, _):
             chunk(i * size, size)
@@ -590,9 +590,9 @@
         if d == depths - 2:
             reduced = start(reduce_copies(0))
     last = start(reduce_copies(1))
+    make_natural()
     wait(reduced)
     casts += cast_image(0)
-    make_natural()
     wait(last)
     casts += cast_image(1)
     wait(casts)

time: 42.6 us -> 42.5 us (level)
  no operation moved by 1% of the time
where the time goes in v7:
time: 42.5 us; the launch traced here: 42.3 us
  Pallas kernels  40.1 us (94%)
  local copies, waits for them, and re-layouts  1.5 us (4%)
  between operations  0.64 us (2%)
    pallas_call x1, Pallas kernels, per_device(): pl.pallas_call(functools.partial(kernel, dims), out_shape=(pltpu.VMEM((de...  40.1 us
    unnamed x2, local copies, waits for them, and re-layouts  1.5 us

profile of v7, /device:TPU:1, one launch (start us, length us, event | category | flops | bytes accessed | tf_op | source)
XLA Modules:
  0.0 42.3 jit_solution(12370126671505149133)
XLA Ops:
  0.6 40.1 %shard_map.41 = (f32[4,128,128]{2,1,0:T(8,128)S(1)}, f32[4,2,128,128]{3,2,1,0:T(8,128)S(1)}) custom-call(f32[4,2,128,128]{3,2,1,0:T(8,128)} %wave_hbm.1, f32[4,16,128]{2,1,0:T(8,128)} %vel_hbm.1), custom_call_target="tpu_custom_call" | custom-call | tf_op jit(solution)/shard_map/pallas_call | solution.py:616
  40.8 0.7 %copy.6 = f32[4,128,128]{2,1,0:T(8,128)} copy(f32[4,128,128]{2,1,0:T(8,128)S(1)} %get-tuple-element.2) | data formatting | bytes 524288
  41.5 0.8 %copy.7 = f32[4,2,128,128]{3,2,1,0:T(8,128)} copy(f32[4,2,128,128]{3,2,1,0:T(8,128)S(1)} %get-tuple-element.3) | data formatting | bytes 1048576

commit v8 on v7

--- a/solution.py
+++ b/solution.py
@@ -482,7 +482,7 @@
                     rows_buf[0, xi, pl.ds(yi0 + j, 8, stride=ny), :] = real[j, xi]
                     rows_buf[1, xi, pl.ds(yi0 + j, 8, stride=ny), :] = imag[j, xi]
 
-        size = 4
+        size = 6
 
         def body(i, _):
             chunk(i * size, size)

time: 42.5 us -> 42.4 us (level)
  no operation moved by 1% of the time
where the time goes in v8:
time: 42.4 us; the launch traced here: 42.2 us
  Pallas kernels  40.1 us (95%)
  local copies, waits for them, and re-layouts  1.5 us (4%)
  between operations  0.64 us (2%)
    pallas_call x1, Pallas kernels, per_device(): pl.pallas_call(functools.partial(kernel, dims), out_shape=(pltpu.VMEM((de...  40.1 us
    unnamed x2, local copies, waits for them, and re-layouts  1.5 us

profile of v8, /device:TPU:1, one launch (start us, length us, event | category | flops | bytes accessed | tf_op | source)
XLA Modules:
  0.0 42.2 jit_solution(2761052367291588384)
XLA Ops:
  0.6 40.1 %shard_map.41 = (f32[4,128,128]{2,1,0:T(8,128)S(1)}, f32[4,2,128,128]{3,2,1,0:T(8,128)S(1)}) custom-call(f32[4,2,128,128]{3,2,1,0:T(8,128)} %wave_hbm.1, f32[4,16,128]{2,1,0:T(8,128)} %vel_hbm.1), custom_call_target="tpu_custom_call" | custom-call | tf_op jit(solution)/shard_map/pallas_call | solution.py:616
  40.7 0.7 %copy.6 = f32[4,128,128]{2,1,0:T(8,128)} copy(f32[4,128,128]{2,1,0:T(8,128)S(1)} %get-tuple-element.2) | data formatting | bytes 524288
  41.4 0.8 %copy.7 = f32[4,2,128,128]{3,2,1,0:T(8,128)} copy(f32[4,2,128,128]{3,2,1,0:T(8,128)S(1)} %get-tuple-element.3) | data formatting | bytes 1048576
